TPU v7x, 128 devices: a whole 4x4x4 slice. The times are simulated.
128 devices in a mesh: attn: 4 (over y), expert: 32 (over z, x, core).
Axes of the slice: x: 4, y: 4, z: 4, core: 2. Of those that a mesh axis runs over, the one named last changes fastest.
Arguments:
- residual: float32 [512, 4096], P('attn', 'expert'), may hold values from -63 to 63
- queries: bfloat16 [512, 8192], P('expert', 'attn'), may hold values from -12 to 12
- keys: bfloat16 [512, 1024, 512], P('expert', None, 'attn'), may hold values from -6 to 6
- values: bfloat16 [512, 1024, 512], P('expert', None, 'attn'), may hold values from -6 to 6
- lengths: int32 [512], P('expert'), may hold values from 1 to 1024, 262144 in all
- out_weight: bfloat16 [8192, 4096], P('attn', 'expert'), may hold values from -0.0625 to 0.0625
- norm_gain: float32 [4096], P('expert'), may hold values from 0.1 to 1.9
- expert_ids: int32 [512, 8], P('attn'), may hold values from 0 to 127, all different within a row; in each aligned block of 128 rows (0 to 127, 128 to 255, ...) at most 16 rows name the same one
- gates: float32 [512, 8], P('attn'), may hold values from 0.05 to 0.5
- gate_up: bfloat16 [128, 4096, 1536], P(('attn', 'expert')), may hold values from -0.09375 to 0.09375
- down: bfloat16 [128, 768, 4096], P(('attn', 'expert')), may hold values from -0.21875 to 0.21875
Outputs:
- layer_out: float32 [512, 4096], P('attn', 'expert')
Inputs may be any that keep to these rules, and one draw needn't show every extreme that they name: `expert_ids`: among the 128 tokens of each index of attn (aligned blocks of rows), no expert is named more than 16 times; a token's 8 experts differ.
All inputs are finite; a program needn't handle non-finite values. No bound on the sum of `lengths` on one device may be relied on, other than what follows from the above.
Results may differ from a plain program's by a relative error of at most 0.0015.
Values may be sent and summed in bfloat16 or wider, within the bound.
A program may use at most 128 MiB of HBM per device.

v0:
```python
import math

import jax
import jax.numpy as jnp
from jax import lax
from jax.sharding import PartitionSpec as P

D = 4096
HD = 128


def expert_apply(rows_in, gate_up_k, down_k):
    mixed = jnp.dot(rows_in, gate_up_k, preferred_element_type=jnp.float32)
    width = down_k.shape[0]
    inner = (jax.nn.silu(mixed[:, :width]) * mixed[:, width:]).astype(jnp.bfloat16)
    return jnp.dot(inner, down_k, preferred_element_type=jnp.float32).astype(jnp.bfloat16)


def run_expert(blocks, gate_up, down):
    shape = blocks.shape
    flat = blocks.reshape(-1, shape[-1])
    produced = expert_apply(flat, gate_up[0], down[0])
    return produced.reshape(shape[:-1] + (down.shape[2],))


def body(
    residual,
    queries,
    keys,
    values,
    lengths,
    out_weight,
    norm_gain,
    expert_ids,
    gates,
    gate_up,
    down,
):
    head_count = queries.shape[1] // HD
    kv_count = keys.shape[2] // HD
    group = head_count // kv_count
    tok_col = queries.shape[0]
    key_span = keys.shape[1]
    query_all = queries.reshape(tok_col, kv_count, group, HD)
    key_all = keys.reshape(tok_col, key_span, kv_count, HD)
    value_all = values.reshape(tok_col, key_span, kv_count, HD)
    scores = jnp.einsum(
        "thgd,tlhd->thgl", query_all, key_all, preferred_element_type=jnp.float32
    ) * (1.0 / math.sqrt(HD))
    valid = (
        jnp.arange(key_span, dtype=jnp.int32)[None, None, None, :] < lengths[:, None, None, None]
    )
    scores = jnp.where(valid, scores, -1e30)
    peak = jnp.max(scores, axis=-1, keepdims=True)
    expo = jnp.where(valid, jnp.exp(scores - peak), 0.0)
    weights = (expo / jnp.sum(expo, axis=-1, keepdims=True)).astype(jnp.bfloat16)
    attended = jnp.einsum("thgl,tlhd->thgd", weights, value_all, preferred_element_type=jnp.float32)
    attended = attended.astype(jnp.bfloat16).reshape(tok_col, head_count * HD)
    projected = jnp.dot(
        lax.all_gather(attended, "expert", axis=0, tiled=True),
        out_weight,
        preferred_element_type=jnp.float32,
    )
    attn_part = lax.psum_scatter(projected, "attn", scatter_dimension=0, tiled=True)
    hidden_state = residual + attn_part
    square = lax.psum(jnp.sum(hidden_state * hidden_state, axis=1), "expert")
    normed = (hidden_state * lax.rsqrt(square / D + 1e-06)[:, None] * norm_gain).astype(
        jnp.bfloat16
    )
    row_count = residual.shape[0]
    top_count = expert_ids.shape[1]
    attn_count = lax.axis_size("attn")
    column_count = lax.axis_size("expert")
    experts = attn_count * column_count
    capacity = max(2, 2 * row_count * top_count // experts)
    flat_ids = expert_ids.reshape(-1)
    onehot = (flat_ids[:, None] == jnp.arange(experts, dtype=jnp.int32)[None, :]).astype(jnp.int32)
    before = jnp.cumsum(onehot, axis=0) - onehot
    slots = jnp.sum(before * onehot, axis=1).reshape(row_count, top_count)
    column = lax.axis_index("expert")
    owners = jnp.arange(attn_count, dtype=jnp.int32) * column_count + column
    matches = expert_ids[None, :, :] == owners[:, None, None]
    slot_hits = slots[None, :, :] == jnp.arange(capacity, dtype=jnp.int32)[:, None, None]
    paired = matches[:, None, :, :] & slot_hits[None, :, :, :]
    select = jnp.any(paired, axis=3).astype(jnp.bfloat16)
    combine = jnp.sum(jnp.where(paired, gates[None, None, :, :], 0.0), axis=3)
    full_rows = lax.all_gather(normed, "expert", axis=1, tiled=True)
    outgoing = jnp.einsum(
        "acr,rd->acd", select, full_rows, preferred_element_type=jnp.float32
    ).astype(jnp.bfloat16)
    returned = lax.all_to_all(
        run_expert(
            lax.all_to_all(outgoing, "attn", split_axis=0, concat_axis=0, tiled=True), gate_up, down
        ),
        "attn",
        split_axis=0,
        concat_axis=0,
        tiled=True,
    )
    partial_value = jnp.einsum(
        "acr,acd->rd", combine, returned.astype(jnp.float32), precision=lax.Precision.HIGHEST
    )
    moe = lax.psum_scatter(partial_value, "expert", scatter_dimension=1, tiled=True)
    return hidden_state + moe


def solution(mesh):
    in_specs = (
        P("attn", "expert"),
        P("expert", "attn"),
        P("expert", None, "attn"),
        P("expert", None, "attn"),
        P("expert"),
        P("attn", "expert"),
        P("expert"),
        P("attn", None),
        P("attn", None),
        P(("attn", "expert"), None, None),
        P(("attn", "expert"), None, None),
    )
    out_specs = P("attn", "expert")
    return jax.shard_map(body, mesh=mesh, in_specs=in_specs, out_specs=out_specs, check_vma=False)
```

profile of v0, /device:TPU:1, one launch (start us, length us, event | category | flops | bytes accessed | tf_op | source)
XLA Modules:
  0.0 313.1 jit_solution(6462457055851880865)
XLA Ops:
  6.5 0.0 copy-start
  6.5 0.0 all-gather.3.cloned.1.call-start
  6.5 0.8 iota_compare_fusion.4
  7.3 0.9 copy.25
  8.2 3.6 %fusion.24 = (f32[16,16]{1,0:T(8,128)S(1)}, f32[16,16,1024]{2,1,0:T(8,128)S(1)}) fusion(pred[16,1024]{1,0:T(8,128)(4,1)S(1)} %iota_compare_fusion.4, bf16[16,16,128]{2,1,0:T(8,128)(2,1)S(1)} %bitcast.44, bf16[16,1024,128]{2,1,0:T(8,128)(2,1)} %param.13), kind=kOutput, calls=%fused_computation.42 | convolution fusion | flops 68420608 | bytes 5325824 | tf_op jit(solution)/shard_map/sub | solution.py:55
  11.8 0.0 copy-start.1
  11.8 0.0 copy-start.4
  11.8 0.0 copy-start.2
  11.8 2.9 convolution_convert_fusion.1
  14.7 0.7 copy.28
  15.4 0.0 all-gather.3.cloned.1.call-update
  15.4 0.0 reduce-scatter.3.cloned.1.call-start
  15.4 47.7 %all-gather.3.cloned.1.call-done = bf16[512,2048]{1,0:T(8,128)(2,1)} async-done(((bf16[16,2048]{1,0:T(8,128)(2,1)}), bf16[512,2048]{1,0:T(8,128)(2,1)}) %all-gather.3.cloned.1.call-update) | async-done | bytes 2097168 | tf_op jit(solution)/shard_map/all_gather | solution.py:60
  63.1 0.0 copy-done
  63.1 3.0 fusion.25
  66.2 0.0 reduce-scatter.3.cloned.1.call-update
  66.2 0.0 all-gather.5.cloned.1.call-start
  66.2 17.3 %reduce-scatter.3.cloned.1.call-done = f32[128,128]{1,0:T(8,128)} async-done(((f32[512,128]{1,0:T(8,128)}), f32[128,128]{1,0:T(8,128)}) %reduce-scatter.3.cloned.1.call-update) | async-done | bytes 65552 | tf_op jit(solution)/shard_map/reduce_scatter | solution.py:64
  83.6 0.0 copy-done.1
  83.6 0.9 multiply_reduce_fusion
  84.5 65.1 %psum.7 = f32[128]{0:T(128)S(1)} all-reduce(f32[128]{0:T(128)S(1)} %get-tuple-element.5), channel_id=1, replica_groups=mesh['attn'=4,'expert'=32] {'expert'}, use_global_device_ids=true, to_apply=%region_9.10 | all-reduce | flops 128 | bytes 1024 | tf_op jit(solution)/shard_map/psum | solution.py:66
  149.6 0.0 copy-done.4
  149.6 0.7 multiply_convert_fusion
  150.3 0.0 all-gather.5.cloned.1.call-update
  150.3 0.0 copy-done.2
  150.3 0.1 copy.20
  150.4 0.1 eq.68
  150.5 0.1 eq.64
  150.6 0.1 copy.22
  150.7 0.2 fusion.15
  151.0 0.1 copy.23
  151.1 0.4 fusion.14
  151.5 0.1 eq.72
  151.6 0.1 broadcast_compare_fusion
  151.7 0.1 and_reduce_fusion
  151.8 39.0 %all-gather.5.cloned.1.call-done = bf16[128,4096]{1,0:T(8,128)(2,1)} async-done(((bf16[128,128]{1,0:T(8,128)(2,1)}), bf16[128,4096]{1,0:T(8,128)(2,1)}) %all-gather.5.cloned.1.call-update) | async-done | bytes 1048592 | tf_op jit(solution)/shard_map/all_gather | solution.py:87
  190.8 1.5 convolution_convert_fusion
  192.4 0.0 slice-start
  192.4 13.1 %all_to_all.10 = bf16[4,16,4096]{2,1,0:T(8,128)(2,1)S(1)} all-to-all(bf16[4,16,4096]{2,1,0:T(8,128)(2,1)S(1)} %convolution_convert_fusion), channel_id=1, replica_groups=mesh['attn'=4,'expert'=32] {'attn'}, dimensions={0} | all-to-all | bytes 1048576 | tf_op jit(solution)/shard_map/all_to_all | solution.py:93
  205.5 0.0 slice-start.1
  205.5 7.0 %fusion.1 = f32[64,1536]{1,0:T(8,128)S(1)} fusion(bf16[64,4096]{1,0:T(8,128)(2,1)S(1)} %bitcast.42, bf16[1,4096,1536]{2,1,0:T(8,128)(2,1)} %param.20), kind=kOutput, calls=%fused_computation.1 | convolution fusion | flops 805306368 | bytes 13500416 | tf_op jit(solution)/shard_map/dot_general | solution.py:13
  212.4 0.0 slice-done
  212.5 0.0 slice-done.1
  212.5 0.0 copy-start.3
  212.5 2.0 fusion.5
  214.5 3.5 %all-to-all-start.1 = ((bf16[4,16,4096]{2,1,0:T(8,128)(2,1)}), bf16[4,16,4096]{2,1,0:T(8,128)(2,1)S(1)}, u32[]{:S(2)}, u32[]{:S(2)}) async-start(bf16[4,16,4096]{2,1,0:T(8,128)(2,1)} %bitcast.7), calls=%async_computation.2 | async-start | bytes 1048576 | tf_op jit(solution)/shard_map/all_to_all | solution.py:91
  218.0 0.0 reduce-scatter.5.cloned.1.call-start
  218.0 0.0 copy-done.3
  218.0 0.1 fusion.18
  218.1 7.6 %all-to-all-done.1 = bf16[4,16,4096]{2,1,0:T(8,128)(2,1)S(1)} async-done(((bf16[4,16,4096]{2,1,0:T(8,128)(2,1)}), bf16[4,16,4096]{2,1,0:T(8,128)(2,1)S(1)}, u32[]{:S(2)}, u32[]{:S(2)}) %all-to-all-start.1) | async-done | bytes 524320 | tf_op jit(solution)/shard_map/all_to_all | solution.py:91
  225.8 2.4 convolution_bitcast_fusion
  228.1 0.0 reduce-scatter.5.cloned.1.call-update
  228.2 76.9 %reduce-scatter.5.cloned.1.call-done = f32[128,128]{1,0:T(8,128)} async-done(((f32[128,4096]{1,0:T(8,128)}), f32[128,128]{1,0:T(8,128)}) %reduce-scatter.5.cloned.1.call-update) | async-done | bytes 65552 | tf_op jit(solution)/shard_map/reduce_scatter | solution.py:103
  305.1 1.5 add.38
  (9 shorter events, 0.2 us)
Async XLA Ops:
  6.5 56.6 %copy-start = (bf16[2048,128]{1,0:T(8,128)(2,1)S(1)}, bf16[2048,128]{1,0:T(8,128)(2,1)}, u32[]{:S(2)}) copy-start(bf16[2048,128]{1,0:T(8,128)(2,1)} %param.16) | copy-start | bytes 1572868
  6.5 56.6 %all-gather.3.cloned.1.call-start = ((), (), s32[]{:S(2)}) async-start(), calls=%async_computation.4 | async-start | bytes 2162688 | tf_op jit(solution)/shard_map/all_gather | solution.py:60
  11.8 71.8 %copy-start.1 = (f32[128,128]{1,0:T(8,128)S(1)}, f32[128,128]{1,0:T(8,128)}, u32[]{:S(2)}) copy-start(f32[128,128]{1,0:T(8,128)} %param.11) | copy-start | bytes 196612
  11.8 137.8 %copy-start.4 = (f32[128]{0:T(128)S(1)}, f32[128]{0:T(128)}, u32[]{:S(2)}) copy-start(f32[128]{0:T(128)} %param.17) | copy-start | bytes 1540
  11.8 138.6 %copy-start.2 = (s32[128,8]{0,1:T(8,128)S(1)}, s32[128,8]{0,1:T(8,128)}, u32[]{:S(2)}) copy-start(s32[128,8]{0,1:T(8,128)} %param.18) | copy-start | bytes 12292
  15.4 68.2 %reduce-scatter.3.cloned.1.call-start = ((), (), s32[]{:S(2)}) async-start(), calls=%async_computation.5 | async-start | bytes 327680 | tf_op jit(solution)/shard_map/reduce_scatter | solution.py:64
  66.2 124.7 %all-gather.5.cloned.1.call-start = ((), (), s32[]{:S(2)}) async-start(), calls=%async_computation.6 | async-start | bytes 1081344 | tf_op jit(solution)/shard_map/all_gather | solution.py:87
  192.4 20.1 %slice-start = ((s8[6291456]{0:T(1024)(128)(4,1)}), s8[4194304]{0:T(1024)(128)(4,1)S(1)}, s32[]{:S(2)}) async-start(s8[6291456]{0:T(1024)(128)(4,1)} %bitcast.40), calls=%async_computation.8 | async-start | bytes 8388608
  205.5 7.0 %slice-start.1 = ((s8[6291456]{0:T(1024)(128)(4,1)}), s8[2097152]{0:T(1024)(128)(4,1)S(1)}, s32[]{:S(2)}) async-start(s8[6291456]{0:T(1024)(128)(4,1)} %bitcast.40), calls=%async_computation.9 | async-start | bytes 4194304
  212.5 5.5 %copy-start.3 = (f32[128,8]{0,1:T(8,128)S(1)}, f32[128,8]{0,1:T(8,128)}, u32[]{:S(2)}) copy-start(f32[128,8]{0,1:T(8,128)} %param.19) | copy-start | bytes 12292
  214.5 11.3 %all-to-all-start.1 = ((bf16[4,16,4096]{2,1,0:T(8,128)(2,1)}), bf16[4,16,4096]{2,1,0:T(8,128)(2,1)S(1)}, u32[]{:S(2)}, u32[]{:S(2)}) async-start(bf16[4,16,4096]{2,1,0:T(8,128)(2,1)} %bitcast.7), calls=%async_computation.2 | async-start | bytes 1048576 | tf_op jit(solution)/shard_map/all_to_all | solution.py:91
  218.0 87.1 %reduce-scatter.5.cloned.1.call-start = ((), (), s32[]{:S(2)}) async-start(), calls=%async_computation.7 | async-start | bytes 2162688 | tf_op jit(solution)/shard_map/reduce_scatter | solution.py:103
Sparse Core Ops, SparseCore 0:
  15.5 47.5 all-gather.2
  66.3 17.1 reduce-scatter.2
  150.4 40.3 all-gather.4
  228.3 76.7 reduce-scatter.4
where the time goes:
time: 314 us; the launch traced here: 313 us
  waiting for transfers between devices  189 us (60%)
  blocking collectives  78.2 us (25%)
  matrix products  22.4 us (7%)
  between operations  13.3 us (4%)
  other arithmetic  4.85 us (2%)
  starting transfers between devices  3.6 us (1%)
    reduce_scatter x1, waiting for transfers between devices, body(): lax.psum_scatter(partial_value, 'expert', scatter_dimension=1, tiled=True)  76.9 us
    psum x1, blocking collectives, body(): square = lax.psum(jnp.sum(hidden_state * hidden_state, axis=1), 'expert')  65.1 us
    all_gather x1, waiting for transfers between devices, body(): lax.all_gather(attended, 'expert', axis=0, tiled=True)  47.7 us
    all_gather x1, waiting for transfers between devices, body(): full_rows = lax.all_gather(normed, 'expert', axis=1, tiled=True)  39 us
    reduce_scatter x1, waiting for transfers between devices, body(): lax.psum_scatter(projected, 'attn', scatter_dimension=0, tiled=True)  17.3 us
    all_to_all x1, blocking collectives, body(): lax.all_to_all(outgoing, 'attn', split_axis=0, concat_axis=0, tiled=True)  13.1 us
    all_to_all x1, waiting for transfers between devices, body(): lax.all_to_all(run_expert(lax.all_to_all(outgoing, 'attn', split_axis=0,...  7.62 us
    dot_general x1, matrix products, expert_apply(): mixed = jnp.dot(rows_in, gate_up_k, preferred_element_type=jnp.float32)  6.96 us
  transfers between devices with their start and end apart: 5, of which 5 were waited for; matrix products, arithmetic and copies ran while one was open for 0% of the time, Pallas kernels for 0%

commit v1 on v0

v1 whole, which is shorter than its diff:
```python
import functools
import math

import jax
import jax.numpy as jnp
from jax import lax
from jax.experimental import pallas as pl
from jax.experimental.pallas import tpu as pltpu
from jax.sharding import PartitionSpec as P

HD = 128
CAP = 16
CORES = 2
PARTS = 3
F32 = jnp.float32
BF16 = jnp.bfloat16
MESH = pl.DeviceIdType.MESH
NT = (((1,), (1,)), ((), ()))


def dot(left, right):
    return jnp.dot(left, right, preferred_element_type=F32)


def dot_nt(left, right):
    return lax.dot_general(left, right, NT, preferred_element_type=F32)


def split3(value):
    high = value.astype(BF16)
    rest = value - high.astype(F32)
    middle = rest.astype(BF16)
    low = (rest - middle.astype(F32)).astype(BF16)
    return high, middle, low


def layer_kernel(
    cfg,
    lengths,
    residual,
    queries,
    keys,
    values,
    out_weight,
    gain,
    ids,
    gates,
    gate_up,
    down,
    out,
    q_in,
    q_rows,
    o_rows,
    k_buf,
    v_buf,
    w_buf,
    res_buf,
    gain_buf,
    ids_all,
    gates_all,
    att,
    part_send,
    part_recv,
    normed,
    select,
    comb_high,
    comb_low,
    x_send,
    x_recv,
    gate_up_buf,
    down_buf,
    mixed,
    y_send,
    y_recv,
    moe_send,
    moe_recv,
    in_sem,
    k_sem,
    v_sem,
    gate_sem,
    w_send,
    w_recv,
    ids_send,
    ids_recv,
    gates_send,
    gates_recv,
    att_send,
    att_recv,
    rs_send,
    rs_recv,
    norm_send,
    norm_recv,
    xs_sem,
    xr_sem,
    ys_sem,
    yr_sem,
    ms_sem,
    mr_sem,
):
    n_attn, n_z, n_x, req, heads, width = cfg
    n_exp = n_z * n_x * CORES
    chips = n_z * n_x
    per_z = n_x * CORES
    block = per_z * req
    half = n_x * req
    features = n_exp * HD
    slots = n_exp * CAP
    rows = n_attn * CAP
    a = lax.axis_index("attn")
    e = lax.axis_index("expert")
    core = lax.rem(e, CORES)
    chip = lax.div(e, CORES)
    x = lax.rem(chip, n_x)
    z = lax.div(chip, n_x)
    sibling = chip * CORES + (1 - core)

    def wrap(value, size):
        return lax.rem(value, size)

    barrier = pltpu.get_barrier_semaphore()

    def greet(d, carry):
        pl.semaphore_signal(
            barrier, inc=1, device_id=(a, wrap(e + d, n_exp)), device_id_type=MESH
        )
        return carry

    lax.fori_loop(1, n_exp, greet, 0)
    for i in range(1, n_attn):
        for other in range(CORES):
            pl.semaphore_signal(
                barrier,
                inc=1,
                device_id=(wrap(a + i, n_attn), chip * CORES + other),
                device_id_type=MESH,
            )

    group = k_buf.shape[0] // k_sem.shape[0]
    n_group = k_sem.shape[0]
    load_q = pltpu.make_async_copy(queries, q_in, in_sem.at[0])
    load_q.start()

    def load_k(g):
        span = pl.ds(g * group, group)
        return pltpu.make_async_copy(keys.at[span], k_buf.at[span], k_sem.at[g])

    def load_v(g):
        span = pl.ds(g * group, group)
        return pltpu.make_async_copy(values.at[span], v_buf.at[span], v_sem.at[g])

    for g in range(n_group):
        load_k(g).start()
        load_v(g).start()
    own_columns = pl.ds(pl.multiple_of(core * HD, HD), HD)
    load_w = pltpu.make_async_copy(out_weight, w_buf.at[:, own_columns], in_sem.at[1])
    load_res = pltpu.make_async_copy(residual, res_buf, in_sem.at[2])
    load_gain = pltpu.make_async_copy(gain, gain_buf, in_sem.at[3])
    load_ids = pltpu.make_async_copy(ids, ids_all.at[a], in_sem.at[4])
    load_gates = pltpu.make_async_copy(gates, gates_all.at[a], in_sem.at[5])
    for load in (load_w, load_res, load_gain, load_ids, load_gates):
        load.start()

    load_q.wait()
    pairs = (heads * req, heads * req)
    first = lax.broadcasted_iota(jnp.int32, pairs, 0)
    second = lax.broadcasted_iota(jnp.int32, pairs, 1)
    by_request = (lax.div(first, heads) == lax.rem(second, req)) & (
        lax.rem(first, heads) == lax.div(second, req)
    )
    stacked = jnp.concatenate([q_in[:, h * HD : (h + 1) * HD] for h in range(heads)], axis=0)
    q_rows[...] = dot(by_request.astype(F32).astype(BF16), stacked).astype(BF16)
    span = k_buf.shape[1]
    position = lax.broadcasted_iota(jnp.int32, (heads, span), 1)
    for g in range(n_group):
        load_k(g).wait()
        load_v(g).wait()
        for i in range(g * group, (g + 1) * group):
            query = q_rows[i * heads : (i + 1) * heads, :]
            scores = dot_nt(query, k_buf[i]) * (1.0 / math.sqrt(HD))
            scores = jnp.where(position < lengths[i], scores, -1e30)
            peak = jnp.max(scores, axis=1, keepdims=True)
            expo = jnp.exp(scores - peak)
            weights = (expo / jnp.sum(expo, axis=1, keepdims=True)).astype(BF16)
            o_rows[i * heads : (i + 1) * heads, :] = dot(weights, v_buf[i]).astype(BF16)
    by_head = (lax.div(first, req) == lax.rem(second, heads)) & (
        lax.rem(first, req) == lax.div(second, heads)
    )
    own = dot(by_head.astype(F32).astype(BF16), o_rows[...])
    att[z, x] = own.astype(BF16).reshape(heads, req, HD)

    pl.semaphore_wait(barrier, n_exp - 1 + CORES * (n_attn - 1))

    def push_att(d):
        to = wrap(chip + d, chips)
        return pltpu.make_async_remote_copy(
            src_ref=att.at[z, x],
            dst_ref=att.at[z, x],
            send_sem=att_send.at[d],
            recv_sem=att_recv.at[chip],
            device_id=(a, to * CORES + core),
            device_id_type=MESH,
        )

    def start_att(d, carry):
        push_att(d).start()
        return carry

    lax.fori_loop(1, chips, start_att, 0)

    push_w = pltpu.make_async_remote_copy(
        src_ref=out_weight,
        dst_ref=w_buf.at[:, own_columns],
        send_sem=w_send,
        recv_sem=w_recv,
        device_id=(a, sibling),
        device_id_type=MESH,
    )
    push_w.start()

    def push_ids(i):
        return pltpu.make_async_remote_copy(
            src_ref=ids,
            dst_ref=ids_all.at[a],
            send_sem=ids_send.at[i],
            recv_sem=ids_recv.at[a],
            device_id=(wrap(a + i, n_attn), e),
            device_id_type=MESH,
        )

    def push_gates(i):
        return pltpu.make_async_remote_copy(
            src_ref=gates,
            dst_ref=gates_all.at[a],
            send_sem=gates_send.at[i],
            recv_sem=gates_recv.at[a],
            device_id=(wrap(a + i, n_attn), e),
            device_id_type=MESH,
        )

    for i in range(1, n_attn):
        push_ids(i).start()
        push_gates(i).start()

    depth = per_z * HD

    def load_gate_up(g):
        part = pl.ds(pl.multiple_of(g * depth, depth), depth)
        return pltpu.make_async_copy(
            gate_up.at[0, part, :], gate_up_buf.at[part, :], gate_sem.at[g]
        )

    load_down = pltpu.make_async_copy(down.at[0], down_buf, in_sem.at[6])
    for g in range(n_z):
        load_gate_up(g).start()
    load_down.start()

    for load in (load_ids, load_gates):
        load.wait()
    earlier = (
        lax.broadcasted_iota(jnp.int32, (block, block), 0)
        < lax.broadcasted_iota(jnp.int32, (block, block), 1)
    ).astype(F32).astype(BF16)
    spread_row = lax.broadcasted_iota(jnp.int32, (slots, n_exp), 0)
    spread_col = lax.broadcasted_iota(jnp.int32, (slots, n_exp), 1)
    spread = (
        ((spread_row >= spread_col * CAP) & (spread_row < (spread_col + 1) * CAP))
        .astype(F32)
        .astype(BF16)
    )
    slot = lax.rem(lax.broadcasted_iota(jnp.int32, (slots, block), 0), CAP).astype(F32)
    named = lax.broadcasted_iota(jnp.int32, (n_exp, block), 0) + a * n_exp
    top = ids_all.shape[1]
    for i in range(n_attn):
        b = wrap(a + i, n_attn)
        if i > 0:
            pltpu.make_async_copy(ids, ids_all.at[b], ids_recv.at[b]).wait()
            pltpu.make_async_copy(gates, gates_all.at[b], gates_recv.at[b]).wait()
        ids_b = ids_all[b]
        gates_b = gates_all[b]
        chosen = jnp.zeros((n_exp, block), F32)
        weight = jnp.zeros((n_exp, block), F32)
        for k in range(top):
            hit = ids_b[k : k + 1, :] == named
            chosen = chosen + jnp.where(hit, 1.0, 0.0)
            weight = weight + jnp.where(hit, gates_b[k : k + 1, :], 0.0)
        rank = dot(chosen.astype(BF16), earlier)
        high = weight.astype(BF16)
        low = (weight - high.astype(F32)).astype(BF16)
        table = jnp.concatenate([rank.astype(BF16), chosen.astype(BF16), high, low], axis=1)
        wide = dot(spread, table)
        here = wide[:, :block] == slot
        select[b] = jnp.where(here, wide[:, block : 2 * block], 0.0).astype(BF16)
        comb_high[b] = jnp.where(here, wide[:, 2 * block : 3 * block], 0.0).T.astype(BF16)
        comb_low[b] = jnp.where(here, wide[:, 3 * block :], 0.0).T.astype(BF16)

    load_w.wait()
    push_w.wait_recv()

    def push_part(i, other):
        return pltpu.make_async_remote_copy(
            src_ref=part_send.at[i, other],
            dst_ref=part_recv.at[a, core],
            send_sem=rs_send.at[i * CORES + other],
            recv_sem=rs_recv.at[a * CORES + core],
            device_id=(wrap(a + i, n_attn), chip * CORES + other),
            device_id_type=MESH,
        )

    for i in [*range(1, n_attn), 0]:
        b = wrap(a + i, n_attn)
        for xx in range(n_x):
            @pl.when(jnp.logical_not((b == z) & (x == xx)))
            def _():
                pltpu.make_async_copy(
                    att.at[b, xx], att.at[b, xx], att_recv.at[b * n_x + xx]
                ).wait()

        left = jnp.concatenate(
            [att[b, :, h].reshape(half, HD) for h in range(heads)], axis=1
        )
        part = dot(left, w_buf[...])
        for other in range(CORES):
            part_send[i, other] = part[:, other * HD : (other + 1) * HD]
        if i > 0:
            for other in range(CORES):
                push_part(i, other).start()
        else:
            push_part(0, 1 - core).start()
            part_recv[a, core] = part_send[0, core]

    for i in range(n_attn):
        b = wrap(a + i, n_attn)
        for other in range(CORES):
            def arrived(b=b, other=other):
                pltpu.make_async_copy(
                    part_recv.at[b, other],
                    part_recv.at[b, other],
                    rs_recv.at[b * CORES + other],
                ).wait()

            if i > 0:
                arrived()
            else:
                pl.when(core != other)(arrived)

    load_res.wait()
    load_gain.wait()
    totals = []
    for other in range(CORES):
        total = part_recv[0, other]
        for b in range(1, n_attn):
            total = total + part_recv[b, other]
        totals.append(total)
    state = res_buf[...] + jnp.concatenate(
        [totals[other][xx * req : (xx + 1) * req] for xx in range(n_x) for other in range(CORES)],
        axis=0,
    )
    square = jnp.sum((state * state).T, axis=0, keepdims=True)
    pieces = split3(square)
    place = lax.broadcasted_iota(jnp.int32, (CAP, block), 0) - PARTS * a
    extra = jnp.zeros((CAP, block), F32)
    for p in range(PARTS):
        extra = extra + jnp.where(place == p, pieces[p].astype(F32), 0.0)
    normed[a, :block, :] = (state * gain_buf[...]).astype(BF16)
    normed[a, block:, :] = extra.astype(BF16)

    def push_norm(i):
        return pltpu.make_async_remote_copy(
            src_ref=normed.at[a],
            dst_ref=normed.at[a],
            send_sem=norm_send.at[i],
            recv_sem=norm_recv.at[a],
            device_id=(wrap(a + i, n_attn), e),
            device_id_type=MESH,
        )

    for i in range(1, n_attn):
        push_norm(i).start()

    squares = jnp.zeros((slots, HD), F32)
    blank = jnp.zeros((HD - CAP, block), F32)
    for i in range(n_attn):
        b = wrap(a + i, n_attn)
        if i > 0:
            pltpu.make_async_copy(normed.at[b], normed.at[b], norm_recv.at[b]).wait()
        beside = jnp.concatenate([normed[b, block:, :].astype(F32), blank], axis=0).T
        both = jnp.concatenate([normed[b, :block, :], beside.astype(BF16)], axis=1)
        picked = dot(select[b], both)
        x_send[:, b] = picked[:, :HD].astype(BF16).reshape(n_exp, CAP, HD)
        squares = squares + picked[:, HD:]
    x_send[:, n_attn] = squares.astype(BF16).reshape(n_exp, CAP, HD)

    def push_x(d):
        to = wrap(e + d, n_exp)
        return pltpu.make_async_remote_copy(
            src_ref=x_send.at[to],
            dst_ref=x_recv.at[e],
            send_sem=xs_sem.at[d],
            recv_sem=xr_sem.at[e],
            device_id=(a, to),
            device_id_type=MESH,
        )

    def start_x(d, carry):
        push_x(d).start()
        return carry

    lax.fori_loop(1, n_exp, start_x, 0)
    x_recv[e] = x_send[e]

    for i in range(n_z):
        zz = wrap(z + i, n_z)
        for q in range(per_z):
            source = zz * per_z + q

            def arrived(source=source):
                pltpu.make_async_copy(
                    x_recv.at[source], x_recv.at[source], xr_sem.at[source]
                ).wait()

            if i > 0:
                arrived()
            else:
                pl.when(source != e)(arrived)
        load_gate_up(zz).wait()
        left = jnp.concatenate(
            [x_recv[zz * per_z + q, :n_attn].reshape(rows, HD) for q in range(per_z)], axis=1
        )
        product = dot(left, gate_up_buf[pl.ds(pl.multiple_of(zz * depth, depth), depth), :])
        if i == 0:
            mixed[...] = product
        else:
            mixed[...] += product

    total = jnp.zeros((CAP, HD), F32)
    for source in range(n_exp):
        total = total + x_recv[source, n_attn].astype(F32)
    scale = jnp.concatenate(
        [
            lax.rsqrt(
                jnp.sum(total[:, PARTS * b : PARTS * (b + 1)], axis=1, keepdims=True) / features
                + 1e-06
            )
            for b in range(n_attn)
        ],
        axis=0,
    )
    gate = mixed[:, :width] * scale
    up = mixed[:, width:] * scale
    inner = (gate / (1.0 + jnp.exp(-gate)) * up).astype(BF16)

    load_down.wait()

    def push_y(to):
        return pltpu.make_async_remote_copy(
            src_ref=y_send.at[to],
            dst_ref=y_recv.at[e],
            send_sem=ys_sem.at[to],
            recv_sem=yr_sem.at[e],
            device_id=(a, to),
            device_id_type=MESH,
        )

    for i in [*range(1, n_z), 0]:
        zz = wrap(z + i, n_z)
        produced = dot(
            inner, down_buf[:, pl.ds(pl.multiple_of(zz * depth, depth), depth)]
        ).astype(BF16)
        for q in range(per_z):
            to = zz * per_z + q
            y_send[to] = produced[:, q * HD : (q + 1) * HD].reshape(n_attn, CAP, HD)

            def leave(to=to):
                push_y(to).start()

            if i > 0:
                leave()
            else:
                pl.when(to != e)(leave)
    y_recv[e] = y_send[e]

    for source in range(n_exp):
        @pl.when(e != source)
        def _():
            pltpu.make_async_copy(
                y_recv.at[source], y_recv.at[source], yr_sem.at[source]
            ).wait()

    def push_moe(i):
        return pltpu.make_async_remote_copy(
            src_ref=moe_send.at[i],
            dst_ref=moe_recv.at[a],
            send_sem=ms_sem.at[i],
            recv_sem=mr_sem.at[a],
            device_id=(wrap(a + i, n_attn), e),
            device_id_type=MESH,
        )

    for i in [*range(1, n_attn), 0]:
        b = wrap(a + i, n_attn)
        back = y_recv[:, b].reshape(slots, HD)
        share = dot(comb_high[b], back) + dot(comb_low[b], back)
        if i > 0:
            moe_send[i] = share
            push_moe(i).start()
        else:
            state = state + share
    for i in range(1, n_attn):
        b = wrap(a + i, n_attn)
        pltpu.make_async_copy(moe_recv.at[b], moe_recv.at[b], mr_sem.at[b]).wait()
        state = state + moe_recv[b]
    out[...] = state

    def end_att(d, carry):
        push_att(d).wait_send()
        return carry

    lax.fori_loop(1, chips, end_att, 0)

    def end_x(d, carry):
        push_x(d).wait_send()
        return carry

    lax.fori_loop(1, n_exp, end_x, 0)

    def end_y(d, carry):
        push_y(wrap(e + d, n_exp)).wait_send()
        return carry

    lax.fori_loop(1, n_exp, end_y, 0)
    push_w.wait_send()
    for i in range(1, n_attn):
        push_ids(i).wait_send()
        push_gates(i).wait_send()
        push_norm(i).wait_send()
        push_moe(i).wait_send()
        for other in range(CORES):
            push_part(i, other).wait_send()
    push_part(0, 1 - core).wait_send()


def body(
    n_attn,
    n_exp,
    residual,
    queries,
    keys,
    values,
    lengths,
    out_weight,
    norm_gain,
    expert_ids,
    gates,
    gate_up,
    down,
):
    req, span = keys.shape[0], keys.shape[1]
    heads = queries.shape[1] // HD
    width = down.shape[1]
    features = gate_up.shape[1]
    block = residual.shape[0]
    n_z = n_attn
    n_x = n_exp // (CORES * n_z)
    rows = n_attn * CAP
    slots = n_exp * CAP
    half = n_x * req
    groups = 4
    top = expert_ids.shape[1]
    cfg = (n_attn, n_z, n_x, req, heads, width)
    anywhere = pl.BlockSpec(memory_space=pl.ANY)
    vmem = pltpu.VMEM
    sem = pltpu.SemaphoreType.DMA
    return pl.pallas_call(
        functools.partial(layer_kernel, cfg),
        out_shape=jax.ShapeDtypeStruct(residual.shape, F32),
        in_specs=[pl.BlockSpec(memory_space=pltpu.SMEM)] + [anywhere] * 10,
        out_specs=pl.BlockSpec(memory_space=pltpu.VMEM),
        scratch_shapes=[
            vmem(queries.shape, BF16),
            vmem((req * heads, HD), BF16),
            vmem((req * heads, HD), BF16),
            vmem(keys.shape, BF16),
            vmem(values.shape, BF16),
            vmem((heads * HD, CORES * HD), BF16),
            vmem(residual.shape, F32),
            vmem((1, HD), F32),
            vmem((n_attn, top, block), jnp.int32),
            vmem((n_attn, top, block), F32),
            vmem((n_z, n_x, heads, req, HD), BF16),
            vmem((n_attn, CORES, half, HD), F32),
            vmem((n_attn, CORES, half, HD), F32),
            vmem((n_attn, block + CAP, HD), BF16),
            vmem((n_attn, slots, block), BF16),
            vmem((n_attn, block, slots), BF16),
            vmem((n_attn, block, slots), BF16),
            vmem((n_exp, n_attn + 1, CAP, HD), BF16),
            vmem((n_exp, n_attn + 1, CAP, HD), BF16),
            vmem((features, 2 * width), BF16),
            vmem((width, features), BF16),
            vmem((rows, 2 * width), F32),
            vmem((n_exp, n_attn, CAP, HD), BF16),
            vmem((n_exp, n_attn, CAP, HD), BF16),
            vmem((n_attn, block, HD), F32),
            vmem((n_attn, block, HD), F32),
            sem((8,)),
            sem((groups,)),
            sem((groups,)),
            sem((n_z,)),
            sem,
            sem,
            sem((n_attn,)),
            sem((n_attn,)),
            sem((n_attn,)),
            sem((n_attn,)),
            sem((n_z * n_x,)),
            sem((n_z * n_x,)),
            sem((n_attn * CORES,)),
            sem((n_attn * CORES,)),
            sem((n_attn,)),
            sem((n_attn,)),
            sem((n_exp,)),
            sem((n_exp,)),
            sem((n_exp,)),
            sem((n_exp,)),
            sem((n_attn,)),
            sem((n_attn,)),
        ],
        compiler_params=pltpu.CompilerParams(
            collective_id=0, has_side_effects=True, vmem_limit_bytes=58 * 1024 * 1024
        ),
        name="layer",
    )(
        lengths,
        residual,
        queries,
        keys,
        values,
        out_weight,
        norm_gain.reshape(1, HD),
        expert_ids.T,
        gates.T,
        gate_up,
        down,
    )


def solution(mesh):
    in_specs = (
        P("attn", "expert"),
        P("expert", "attn"),
        P("expert", None, "attn"),
        P("expert", None, "attn"),
        P("expert"),
        P("attn", "expert"),
        P("expert"),
        P("attn", None),
        P("attn", None),
        P(("attn", "expert"), None, None),
        P(("attn", "expert"), None, None),
    )
    run = functools.partial(body, mesh.shape["attn"], mesh.shape["expert"])
    return jax.shard_map(
        run, mesh=mesh, in_specs=in_specs, out_specs=P("attn", "expert"), check_vma=False
    )
```

time: 314 us -> 70.9 us (0.23)
  waiting for transfers between devices: 189 us -> 0 us
  blocking collectives: 78.2 us -> 0 us
  Pallas kernels: 0 us -> 69.3 us
  matrix products: 22.4 us -> 0 us
  between operations: 13.3 us -> 0.01 us
  other arithmetic: 4.85 us -> 0 us
  starting transfers between devices: 3.6 us -> 0 us
    reduce_scatter x2 -> x0, waiting for transfers between devices: 94.2 us -> none  [the longest x1 76.9 us: body(): lax.psum_scatter(partial_value, 'expert', scatter_dimension=1, tiled=True)]
    all_gather x2 -> x0, waiting for transfers between devices: 86.7 us -> none  [the longest x1 47.7 us: body(): lax.all_gather(attended, 'expert', axis=0, tiled=True)]
    pallas_call x0 -> x1, Pallas kernels: none -> 69.3 us  [body(): pl.pallas_call(functools.partial(layer_kernel, cfg), out_shape=jax.ShapeD...]
    psum x1 -> x0, blocking collectives: 65.1 us -> none  [body(): square = lax.psum(jnp.sum(hidden_state * hidden_state, axis=1), 'expert')]
    dot_general x6 -> x0, matrix products: 18.8 us -> none  [the longest x1 6.96 us: expert_apply(): mixed = jnp.dot(rows_in, gate_up_k, preferred_element_type=jnp.float32)]
    all_to_all x1 -> x0, blocking collectives: 13.1 us -> none  [body(): lax.all_to_all(outgoing, 'attn', split_axis=0, concat_axis=0, tiled=True)]
    all_to_all x1 -> x0, waiting for transfers between devices: 7.62 us -> none  [body(): lax.all_to_all(run_expert(lax.all_to_all(outgoing, 'attn', split_axis=0,...]
    sub x1 -> x0, matrix products: 3.56 us -> none  [body(): expo = jnp.where(valid, jnp.exp(scores - peak), 0.0)]
  transfers between devices with their start and end apart: 5 -> 0, of which waited for: 5 -> 0; matrix products, arithmetic and copies ran while one was open for 0% -> 0% of each run, Pallas kernels for 0% -> 0%
where the time goes in v1:
time: 70.9 us; the launch traced here: 70.8 us
  Pallas kernels  69.3 us (98%)
  local copies, waits for them, and re-layouts  1.47 us (2%)
    pallas_call x1, Pallas kernels, body(): pl.pallas_call(functools.partial(layer_kernel, cfg), out_shape=jax.ShapeD...  69.3 us
    unnamed x1, local copies, waits for them, and re-layouts  1.47 us

profile of v1, /device:TPU:1, one launch (start us, length us, event | category | flops | bytes accessed | tf_op | source)
XLA Modules:
  0.0 70.8 jit_solution(10469107035155037029)
XLA Ops:
  0.0 69.3 %layer.1 = f32[128,128]{1,0:T(8,128)} custom-call(s32[16]{0:T(128)} %lengths.1, f32[128,128]{1,0:T(8,128)} %residual.1, bf16[16,2048]{1,0:T(8,128)(2,1)} %queries.1, bf16[16,1024,128]{2,1,0:T(8,128)(2,1)} %keys.1, bf16[16,1024,128]{2,1,0:T(8,128)(2,1)} %values.1, bf16[2048,128]{1,0:T(8,128)(2,1)} %out_weight.1, f32[1,128]{1,0:T(1,128)} %bitcast.5, ...), custom_call_target="tpu_custom_call" | custom-call | tf_op jit(solution)/shard_map/layer/pallas_call | solution.py:573
  69.3 1.5 %copy.13 = f32[128,128]{1,0:T(8,128)} copy(f32[128,128]{1,0:T(8,128)} %layer.1) | data formatting | bytes 131072

commit v2 on v1

v2 whole, which is shorter than its diff:
```python
import functools
import math

import jax
import jax.numpy as jnp
from jax import lax
from jax.experimental import pallas as pl
from jax.experimental.pallas import tpu as pltpu
from jax.sharding import PartitionSpec as P

HD = 128
CAP = 16
CORES = 2
F32 = jnp.float32
BF16 = jnp.bfloat16
MESH = pl.DeviceIdType.MESH
NT = (((1,), (1,)), ((), ()))


def dot(left, right):
    return jnp.dot(left, right, preferred_element_type=F32)


def dot_nt(left, right):
    return lax.dot_general(left, right, NT, preferred_element_type=F32)


def layer_kernel(
    cfg,
    lengths,
    residual,
    queries,
    keys,
    values,
    out_weight,
    gain,
    ids,
    gates,
    gate_up,
    down,
    out,
    q_in,
    q_rows,
    o_rows,
    k_buf,
    v_buf,
    w_buf,
    res_buf,
    gain_all,
    gain_inv,
    ids_buf,
    gates_buf,
    att,
    part_send,
    part_recv,
    select,
    comb_high,
    comb_low,
    x_send,
    x_recv,
    gate_up_buf,
    down_buf,
    mixed,
    y_send,
    y_recv,
    in_sem,
    k_sem,
    v_sem,
    gate_sem,
    w_send,
    w_recv,
    gain_send,
    gain_recv,
    own_send,
    pass_send,
    att_recv,
    rs_send,
    rs_recv,
    xs_sem,
    xr_sem,
    ys_sem,
    yr_sem,
):
    n_attn, n_z, n_x, req, heads, width = cfg
    n_exp = n_z * n_x * CORES
    per_z = n_x * CORES
    block = per_z * req
    half = n_x * req
    features = n_exp * HD
    slots = n_exp * CAP
    rows = n_attn * CAP
    experts = n_attn * n_exp
    split = heads // 2
    a = lax.axis_index("attn")
    e = lax.axis_index("expert")
    core = lax.rem(e, CORES)
    chip = lax.div(e, CORES)
    x = lax.rem(chip, n_x)
    z = lax.div(chip, n_x)
    sibling = chip * CORES + (1 - core)
    mine = a * n_exp + e

    def wrap(value, size):
        return lax.rem(value, size)

    def ring(size):
        return sorted(range(1, size), key=lambda d: min(d, size - d))

    n_group = k_sem.shape[0]
    group = req // n_group
    load_q = pltpu.make_async_copy(queries, q_in, in_sem.at[0])
    load_q.start()

    def load_k(g):
        span = pl.ds(g * group, group)
        return pltpu.make_async_copy(keys.at[span], k_buf.at[span], k_sem.at[g])

    def load_v(g):
        span = pl.ds(g * group, group)
        return pltpu.make_async_copy(values.at[span], v_buf.at[span], v_sem.at[g])

    for g in range(n_group):
        load_k(g).start()
        load_v(g).start()
    own_columns = pl.ds(pl.multiple_of(core * HD, HD), HD)
    load_w = pltpu.make_async_copy(out_weight, w_buf.at[:, own_columns], in_sem.at[1])
    load_res = pltpu.make_async_copy(residual, res_buf, in_sem.at[2])
    load_ids = pltpu.make_async_copy(ids, ids_buf, in_sem.at[3])
    load_gates = pltpu.make_async_copy(gates, gates_buf, in_sem.at[4])
    for load in (load_w, load_res, load_ids, load_gates):
        load.start()

    barrier = pltpu.get_barrier_semaphore()

    def greet(d, carry):
        pl.semaphore_signal(
            barrier, inc=1, device_id=(a, wrap(e + d, n_exp)), device_id_type=MESH
        )
        return carry

    lax.fori_loop(1, n_exp, greet, 0)
    for i in range(1, n_attn):
        for other in range(CORES):
            pl.semaphore_signal(
                barrier,
                inc=1,
                device_id=(wrap(a + i, n_attn), chip * CORES + other),
                device_id_type=MESH,
            )

    load_q.wait()
    pairs = (heads * req, heads * req)
    first = lax.broadcasted_iota(jnp.int32, pairs, 0)
    second = lax.broadcasted_iota(jnp.int32, pairs, 1)
    by_request = (lax.div(first, heads) == lax.rem(second, req)) & (
        lax.rem(first, heads) == lax.div(second, req)
    )
    stacked = jnp.concatenate([q_in[:, h * HD : (h + 1) * HD] for h in range(heads)], axis=0)
    q_rows[...] = dot(by_request.astype(F32).astype(BF16), stacked).astype(BF16)
    span = k_buf.shape[1]
    position = lax.broadcasted_iota(jnp.int32, (heads, span), 1)

    def score(g):
        load_k(g).wait()
        return [
            dot_nt(q_rows[i * heads : (i + 1) * heads, :], k_buf[i])
            for i in range(g * group, (g + 1) * group)
        ]

    ahead = score(0)
    for g in range(n_group):
        scores = ahead
        if g + 1 < n_group:
            ahead = score(g + 1)
        weights = []
        for j in range(group):
            masked = jnp.where(
                position < lengths[g * group + j], scores[j] * (1.0 / math.sqrt(HD)), -1e30
            )
            expo = jnp.exp(masked - jnp.max(masked, axis=1, keepdims=True))
            weights.append((expo / jnp.sum(expo, axis=1, keepdims=True)).astype(BF16))
        load_v(g).wait()
        results = [dot(weights[j], v_buf[g * group + j]).astype(BF16) for j in range(group)]
        o_rows[g * group * heads : (g + 1) * group * heads, :] = jnp.concatenate(results, axis=0)
    by_head = (lax.div(first, req) == lax.rem(second, heads)) & (
        lax.rem(first, req) == lax.div(second, heads)
    )
    own = dot(by_head.astype(F32).astype(BF16), o_rows[...]).astype(BF16)
    for part in range(2):
        att[part, z, x] = own[part * split * req : (part + 1) * split * req].reshape(
            split, req, HD
        )

    pl.semaphore_wait(barrier, n_exp - 1 + CORES * (n_attn - 1))

    def along_x(part, item_z, item_x, d, sem):
        return pltpu.make_async_remote_copy(
            src_ref=att.at[part, item_z, item_x],
            dst_ref=att.at[part, item_z, item_x],
            send_sem=sem,
            recv_sem=att_recv.at[part, item_z, item_x],
            device_id=(a, (z * n_x + wrap(x + d, n_x)) * CORES + core),
            device_id_type=MESH,
        )

    def along_z(part, item_z, item_x, d, sem):
        return pltpu.make_async_remote_copy(
            src_ref=att.at[part, item_z, item_x],
            dst_ref=att.at[part, item_z, item_x],
            send_sem=sem,
            recv_sem=att_recv.at[part, item_z, item_x],
            device_id=(a, (wrap(z + d, n_z) * n_x + x) * CORES + core),
            device_id_type=MESH,
        )

    def att_arrived(part, item_z, item_x):
        item = att.at[part, item_z, item_x]
        pltpu.make_async_copy(item, item, att_recv.at[part, item_z, item_x]).wait()

    sends = []
    for part in (0, 1):
        for k, d in enumerate(ring(n_x)):
            sends.append(("x", part, k, d))
        for k, d in enumerate(ring(n_z)):
            sends.append(("z", part, k, d))
    order = [c for c in sends if (c[0] == "x") == (c[1] == 0)]
    order += [c for c in sends if (c[0] == "x") != (c[1] == 0)]

    def own_copy(c):
        axis, part, k, d = c
        if axis == "x":
            return along_x(part, z, x, d, own_send.at[part, k])
        return along_z(part, z, x, d, own_send.at[part, n_x - 1 + k])

    for c in order:
        own_copy(c).start()

    push_w = pltpu.make_async_remote_copy(
        src_ref=out_weight,
        dst_ref=w_buf.at[:, own_columns],
        send_sem=w_send,
        recv_sem=w_recv,
        device_id=(a, sibling),
        device_id_type=MESH,
    )
    push_w.start()

    depth = per_z * HD

    def load_gate_up(g):
        part = pl.ds(pl.multiple_of(g * depth, depth), depth)
        return pltpu.make_async_copy(
            gate_up.at[0, part, :], gate_up_buf.at[part, :], gate_sem.at[g]
        )

    load_down = pltpu.make_async_copy(down.at[0], down_buf, in_sem.at[5])
    for g in range(n_z):
        load_gate_up(g).start()
    load_down.start()

    own_gain = pltpu.make_async_copy(gain, gain_all.at[e], gain_recv)
    own_gain.start()

    def push_gain(d):
        return pltpu.make_async_remote_copy(
            src_ref=gain,
            dst_ref=gain_all.at[e],
            send_sem=gain_send.at[d],
            recv_sem=gain_recv,
            device_id=(a, wrap(e + d, n_exp)),
            device_id_type=MESH,
        )

    def start_gain(d, carry):
        push_gain(d).start()
        return carry

    lax.fori_loop(1, n_exp, start_gain, 0)

    passes = []
    for k in range(max(n_x, n_z) - 1):
        if k < n_x - 1:
            from_x = wrap(x + ring(n_x)[k], n_x)
            att_arrived(0, z, from_x)
            for m, d in enumerate(ring(n_z)):
                copy = along_z(0, z, from_x, d, pass_send.at[0, k, m])
                copy.start()
                passes.append(copy)
        if k < n_z - 1:
            from_z = wrap(z + ring(n_z)[k], n_z)
            att_arrived(1, from_z, x)
            for m, d in enumerate(ring(n_x)):
                copy = along_x(1, from_z, x, d, pass_send.at[1, k, m])
                copy.start()
                passes.append(copy)

    load_ids.wait()
    load_gates.wait()
    earlier = (
        lax.broadcasted_iota(jnp.int32, (block, block), 0)
        < lax.broadcasted_iota(jnp.int32, (block, block), 1)
    ).astype(F32).astype(BF16)
    spread_row = lax.broadcasted_iota(jnp.int32, (slots, n_exp), 0)
    spread_col = lax.broadcasted_iota(jnp.int32, (slots, n_exp), 1)
    spread = (
        ((spread_row >= spread_col * CAP) & (spread_row < (spread_col + 1) * CAP))
        .astype(F32)
        .astype(BF16)
    )
    slot = lax.rem(lax.broadcasted_iota(jnp.int32, (slots, block), 0), CAP).astype(F32)
    local = lax.broadcasted_iota(jnp.int32, (n_exp, block), 0)
    for p in range(n_attn):
        named = local + p * n_exp
        chosen = jnp.zeros((n_exp, block), F32)
        weight = jnp.zeros((n_exp, block), F32)
        for k in range(ids_buf.shape[0]):
            hit = ids_buf[k : k + 1, :] == named
            chosen = chosen + jnp.where(hit, 1.0, 0.0)
            weight = weight + jnp.where(hit, gates_buf[k : k + 1, :], 0.0)
        rank = dot(chosen.astype(BF16), earlier)
        high = weight.astype(BF16)
        low = (weight - high.astype(F32)).astype(BF16)
        table = jnp.concatenate([rank.astype(BF16), chosen.astype(BF16), high, low], axis=1)
        wide = dot(spread, table)
        here = wide[:, :block] == slot
        select[p] = jnp.where(here, wide[:, block : 2 * block], 0.0).astype(BF16)
        comb_high[p] = jnp.where(here, wide[:, 2 * block : 3 * block], 0.0).T.astype(BF16)
        comb_low[p] = jnp.where(here, wide[:, 3 * block :], 0.0).T.astype(BF16)

    pltpu.make_async_copy(gain_all, gain_all, gain_recv).wait()
    gain_inv[...] = 1.0 / gain_all[...]

    load_w.wait()
    push_w.wait_recv()

    def push_part(b, other):
        return pltpu.make_async_remote_copy(
            src_ref=part_send.at[b, other],
            dst_ref=part_recv.at[a, core],
            send_sem=rs_send.at[b * CORES + other],
            recv_sem=rs_recv.at[a * CORES + core],
            device_id=(b, chip * CORES + other),
            device_id_type=MESH,
        )

    for i in [0, *ring(n_z)]:
        b = wrap(z + i, n_z)
        for d in ring(n_x):
            if i > 0:
                att_arrived(0, b, wrap(x + d, n_x))
            att_arrived(1, b, wrap(x + d, n_x))
        if i > 0:
            att_arrived(0, b, x)
        left = jnp.concatenate(
            [att[h // split, b, :, h % split].reshape(half, HD) for h in range(heads)], axis=1
        )
        product = dot(left, w_buf[...])
        for other in range(CORES):
            part_send[b, other] = product[:, other * HD : (other + 1) * HD].astype(BF16)

        @pl.when(b != a)
        def _():
            for other in range(CORES):
                push_part(b, other).start()

        @pl.when(b == a)
        def _():
            push_part(b, 1 - core).start()
            part_recv[a, core] = part_send[b, core]

    for i in range(n_attn):
        b = wrap(a + i, n_attn)
        for other in range(CORES):
            def arrived(b=b, other=other):
                pltpu.make_async_copy(
                    part_recv.at[b, other],
                    part_recv.at[b, other],
                    rs_recv.at[b * CORES + other],
                ).wait()

            if i > 0:
                arrived()
            else:
                pl.when(core != other)(arrived)

    load_res.wait()
    totals = []
    for other in range(CORES):
        total = part_recv[0, other].astype(F32)
        for b in range(1, n_attn):
            total = total + part_recv[b, other].astype(F32)
        totals.append(total)
    state = res_buf[...] + jnp.concatenate(
        [totals[other][xx * req : (xx + 1) * req] for xx in range(n_x) for other in range(CORES)],
        axis=0,
    )
    out[...] = state
    scaled = (state * gain_all[e]).astype(BF16)

    for p in range(n_attn):
        picked = dot(select[p], scaled).astype(BF16)
        x_send[p * n_exp : (p + 1) * n_exp] = picked.reshape(n_exp, CAP, HD)

    def push_x(to_a, to_e):
        return pltpu.make_async_remote_copy(
            src_ref=x_send.at[to_a * n_exp + to_e],
            dst_ref=x_recv.at[e, a],
            send_sem=xs_sem,
            recv_sem=xr_sem.at[z],
            device_id=(to_a, to_e),
            device_id_type=MESH,
        )

    own_x = pltpu.make_async_copy(x_send.at[mine], x_recv.at[e, a], xr_sem.at[z])
    own_x.start()

    def start_x(d, carry):
        for i in [*range(1, n_attn), 0]:
            push_x(wrap(a + i, n_attn), wrap(e + d, n_exp)).start()
        return carry

    lax.fori_loop(1, n_exp, start_x, 0)
    for i in range(1, n_attn):
        push_x(wrap(a + i, n_attn), e).start()

    squares = jnp.zeros((rows, HD), F32)
    for i in [0, *ring(n_z)]:
        zz = wrap(z + i, n_z)
        arrived = x_recv.at[pl.ds(zz * per_z, per_z)]
        pltpu.make_async_copy(arrived, arrived, xr_sem.at[zz]).wait()
        load_gate_up(zz).wait()
        pieces = [x_recv[zz * per_z + q].reshape(rows, HD) for q in range(per_z)]
        for q in range(per_z):
            plain = pieces[q].astype(F32) * gain_inv[zz * per_z + q]
            squares = squares + plain * plain
        left = jnp.concatenate(pieces, axis=1)
        product = dot(left, gate_up_buf[pl.ds(pl.multiple_of(zz * depth, depth), depth), :])
        if i == 0:
            mixed[...] = product
        else:
            mixed[...] += product

    scale = lax.rsqrt(jnp.sum(squares, axis=1, keepdims=True) / features + 1e-06)
    gate = mixed[:, :width] * scale
    up = mixed[:, width:] * scale
    inner = (gate / (1.0 + jnp.exp(-gate)) * up).astype(BF16)

    load_down.wait()

    def push_y(to_a, to_e):
        return pltpu.make_async_remote_copy(
            src_ref=y_send.at[to_e * n_attn + to_a],
            dst_ref=y_recv.at[mine],
            send_sem=ys_sem,
            recv_sem=yr_sem.at[a],
            device_id=(to_a, to_e),
            device_id_type=MESH,
        )

    for i in [*ring(n_z)[::-1], 0]:
        zz = wrap(z + i, n_z)
        produced = dot(
            inner, down_buf[:, pl.ds(pl.multiple_of(zz * depth, depth), depth)]
        ).astype(BF16)
        for q in range(per_z):
            y_send[pl.ds((zz * per_z + q) * n_attn, n_attn)] = produced[
                :, q * HD : (q + 1) * HD
            ].reshape(n_attn, CAP, HD)

        def start_y(q, carry, zz=zz, own=(i == 0)):
            to = zz * per_z + q
            for k in range(1, n_attn):
                push_y(wrap(a + k, n_attn), to).start()
            if own:
                pl.when(to != e)(lambda: push_y(a, to).start())
            else:
                push_y(a, to).start()
            return carry

        lax.fori_loop(0, per_z, start_y, 0)
    own_y = pltpu.make_async_copy(y_send.at[e * n_attn + a], y_recv.at[mine], yr_sem.at[a])
    own_y.start()

    for i in range(n_attn):
        p = wrap(a + i, n_attn)
        arrived = y_recv.at[pl.ds(p * n_exp, n_exp)]
        pltpu.make_async_copy(arrived, arrived, yr_sem.at[p]).wait()
        back = y_recv[pl.ds(p * n_exp, n_exp)].reshape(slots, HD)
        out[...] += dot(comb_high[p], back) + dot(comb_low[p], back)

    for c in order:
        own_copy(c).wait_send()
    for copy in passes:
        copy.wait_send()
    push_w.wait_send()

    def end_gain(d, carry):
        push_gain(d).wait_send()
        return carry

    lax.fori_loop(1, n_exp, end_gain, 0)
    for b in range(n_attn):
        for other in range(CORES):
            def left_here(b=b, other=other):
                push_part(b, other).wait_send()

            pl.when(jnp.logical_not((b == a) & (core == other)))(left_here)
    for buffer, sem in ((x_send, xs_sem), (y_send, ys_sem)):
        gone = buffer.at[pl.ds(0, experts - 1)]
        pltpu.make_async_copy(gone, gone, sem).wait()


def body(
    n_attn,
    n_exp,
    residual,
    queries,
    keys,
    values,
    lengths,
    out_weight,
    norm_gain,
    expert_ids,
    gates,
    gate_up,
    down,
):
    req, span = keys.shape[0], keys.shape[1]
    heads = queries.shape[1] // HD
    width = down.shape[1]
    features = gate_up.shape[1]
    block = residual.shape[0]
    n_z = n_attn
    n_x = n_exp // (CORES * n_z)
    rows = n_attn * CAP
    slots = n_exp * CAP
    half = n_x * req
    groups = 4
    top = expert_ids.shape[1]
    cfg = (n_attn, n_z, n_x, req, heads, width)
    anywhere = pl.BlockSpec(memory_space=pl.ANY)
    vmem = pltpu.VMEM
    sem = pltpu.SemaphoreType.DMA
    return pl.pallas_call(
        functools.partial(layer_kernel, cfg),
        out_shape=jax.ShapeDtypeStruct(residual.shape, F32),
        in_specs=[pl.BlockSpec(memory_space=pltpu.SMEM)] + [anywhere] * 10,
        out_specs=pl.BlockSpec(memory_space=pltpu.VMEM),
        scratch_shapes=[
            vmem(queries.shape, BF16),
            vmem((req * heads, HD), BF16),
            vmem((req * heads, HD), BF16),
            vmem(keys.shape, BF16),
            vmem(values.shape, BF16),
            vmem((heads * HD, CORES * HD), BF16),
            vmem(residual.shape, F32),
            vmem((n_exp, 1, HD), F32),
            vmem((n_exp, 1, HD), F32),
            vmem((top, block), jnp.int32),
            vmem((top, block), F32),
            vmem((2, n_z, n_x, heads // 2, req, HD), BF16),
            vmem((n_attn, CORES, half, HD), BF16),
            vmem((n_attn, CORES, half, HD), BF16),
            vmem((n_attn, slots, block), BF16),
            vmem((n_attn, block, slots), BF16),
            vmem((n_attn, block, slots), BF16),
            vmem((n_attn * n_exp, CAP, HD), BF16),
            vmem((n_exp, n_attn, CAP, HD), BF16),
            vmem((features, 2 * width), BF16),
            vmem((width, features), BF16),
            vmem((rows, 2 * width), F32),
            vmem((n_exp * n_attn, CAP, HD), BF16),
            vmem((n_attn * n_exp, CAP, HD), BF16),
            sem((6,)),
            sem((groups,)),
            sem((groups,)),
            sem((n_z,)),
            sem,
            sem,
            sem((n_exp,)),
            sem,
            sem((2, n_x + n_z - 2)),
            sem((2, max(n_x, n_z) - 1, max(n_x, n_z) - 1)),
            sem((2, n_z, n_x)),
            sem((n_attn * CORES,)),
            sem((n_attn * CORES,)),
            sem,
            sem((n_z,)),
            sem,
            sem((n_attn,)),
        ],
        compiler_params=pltpu.CompilerParams(
            collective_id=0, has_side_effects=True, vmem_limit_bytes=58 * 1024 * 1024
        ),
        name="layer",
    )(
        lengths,
        residual,
        queries,
        keys,
        values,
        out_weight,
        norm_gain.reshape(1, HD),
        expert_ids.T,
        gates.T,
        gate_up,
        down,
    )


def solution(mesh):
    in_specs = (
        P("attn", "expert"),
        P("expert", "attn"),
        P("expert", None, "attn"),
        P("expert", None, "attn"),
        P("expert"),
        P("attn", "expert"),
        P("expert"),
        P("attn", None),
        P("attn", None),
        P(("attn", "expert"), None, None),
        P(("attn", "expert"), None, None),
    )
    run = functools.partial(body, mesh.shape["attn"], mesh.shape["expert"])
    return jax.shard_map(
        run, mesh=mesh, in_specs=in_specs, out_specs=P("attn", "expert"), check_vma=False
    )
```

time: 70.9 us -> 50.9 us (0.72)
  Pallas kernels: 69.3 us -> 49.2 us
    pallas_call x1, Pallas kernels: 69.3 us -> 49.2 us  [body(): pl.pallas_call(functools.partial(layer_kernel, cfg), out_shape=jax.ShapeD...]
where the time goes in v2:
time: 50.9 us; the launch traced here: 50.7 us
  Pallas kernels  49.2 us (97%)
  local copies, waits for them, and re-layouts  1.47 us (3%)
    pallas_call x1, Pallas kernels, body(): pl.pallas_call(functools.partial(layer_kernel, cfg), out_shape=jax.ShapeD...  49.2 us
    unnamed x1, local copies, waits for them, and re-layouts  1.47 us

profile of v2, /device:TPU:1, one launch (start us, length us, event | category | flops | bytes accessed | tf_op | source)
XLA Modules:
  0.0 50.7 jit_solution(5568014329094097369)
XLA Ops:
  0.0 49.2 %layer.1 = f32[128,128]{1,0:T(8,128)} custom-call(s32[16]{0:T(128)} %lengths.1, f32[128,128]{1,0:T(8,128)} %residual.1, bf16[16,2048]{1,0:T(8,128)(2,1)} %queries.1, bf16[16,1024,128]{2,1,0:T(8,128)(2,1)} %keys.1, bf16[16,1024,128]{2,1,0:T(8,128)(2,1)} %values.1, bf16[2048,128]{1,0:T(8,128)(2,1)} %out_weight.1, f32[1,128]{1,0:T(1,128)} %bitcast.5, ...), custom_call_target="tpu_custom_call" | custom-call | tf_op jit(solution)/shard_map/layer/pallas_call | solution.py:544
  49.2 1.5 %copy.13 = f32[128,128]{1,0:T(8,128)} copy(f32[128,128]{1,0:T(8,128)} %layer.1) | data formatting | bytes 131072

commit v3 on v2

v3 whole, which is shorter than its diff:
```python
import functools
import math

import jax
import jax.numpy as jnp
from jax import lax
from jax.experimental import pallas as pl
from jax.experimental.pallas import tpu as pltpu
from jax.sharding import PartitionSpec as P

HD = 128
CAP = 16
CORES = 2
PARTS = 3
F32 = jnp.float32
BF16 = jnp.bfloat16
MESH = pl.DeviceIdType.MESH
NT = (((1,), (1,)), ((), ()))


def dot(left, right):
    return jnp.dot(left, right, preferred_element_type=F32)


def dot_nt(left, right):
    return lax.dot_general(left, right, NT, preferred_element_type=F32)


def layer_kernel(
    cfg,
    lengths,
    residual,
    queries,
    keys,
    values,
    out_weight,
    gain,
    ids,
    gates,
    gate_up,
    down,
    out,
    q_in,
    q_rows,
    o_rows,
    k_buf,
    v_buf,
    w_buf,
    res_buf,
    len_buf,
    gain_buf,
    gain_inv,
    ids_buf,
    gates_buf,
    att,
    part_send,
    part_recv,
    select,
    comb_high,
    comb_low,
    x_send,
    x_recv,
    gate_up_buf,
    down_buf,
    mixed,
    y_send,
    y_recv,
    in_sem,
    k_sem,
    v_sem,
    gate_sem,
    w_send,
    w_recv,
    gain_send,
    gain_recv,
    own_send,
    pass_send,
    att_recv,
    rs_send,
    rs_recv,
    xs_sem,
    xr_sem,
    ys_sem,
    yr_sem,
):
    n_attn, n_z, n_x, req, heads, width = cfg
    n_exp = n_z * n_x * CORES
    per_z = n_x * CORES
    block = per_z * req
    half = n_x * req
    features = n_exp * HD
    slots = n_exp * CAP
    rows = n_attn * CAP
    experts = n_attn * n_exp
    part_req = req // 2
    couples = heads // 2
    far = [n_z // 2, *(d for d in range(1, n_z) if d != n_z // 2), 0]
    a = lax.axis_index("attn")
    e = lax.axis_index("expert")
    core = lax.rem(e, CORES)
    chip = lax.div(e, CORES)
    x = lax.rem(chip, n_x)
    z = lax.div(chip, n_x)
    sibling = chip * CORES + (1 - core)
    lane = lax.rem(e, per_z)

    def wrap(value, size):
        return lax.rem(value, size)

    def ring(size):
        return sorted(range(1, size), key=lambda d: min(d, size - d))

    n_group = k_sem.shape[0]
    group = req // n_group
    load_q = pltpu.make_async_copy(queries, q_in, in_sem.at[8])
    load_len = pltpu.make_async_copy(lengths, len_buf, in_sem.at[6])
    load_q.start()
    load_len.start()

    def load_k(g):
        span = pl.ds(g * group, group)
        return pltpu.make_async_copy(keys.at[span], k_buf.at[span], k_sem.at[g])

    def load_v(g):
        span = pl.ds(g * group, group)
        return pltpu.make_async_copy(values.at[span], v_buf.at[span], v_sem.at[g])

    for g in range(n_group):
        load_k(g).start()
        load_v(g).start()

    def load_w(q):
        return pltpu.make_async_copy(out_weight.at[:, q], w_buf.at[q, core], in_sem.at[q])

    load_gain = pltpu.make_async_copy(gain, gain_buf, in_sem.at[7])
    load_res = pltpu.make_async_copy(residual, res_buf, in_sem.at[2])
    load_ids = pltpu.make_async_copy(ids, ids_buf, in_sem.at[3])
    load_gates = pltpu.make_async_copy(gates, gates_buf, in_sem.at[4])
    for load in (load_gain, load_res, load_ids, load_gates, load_w(0), load_w(1)):
        load.start()

    barrier = pltpu.get_barrier_semaphore()
    known = [(a, (z * n_x + wrap(x + d, n_x)) * CORES + core) for d in range(1, n_x)]
    known += [(a, (wrap(z + d, n_z) * n_x + x) * CORES + core) for d in range(1, n_z)]
    known += [(a, sibling)]
    known += [
        (wrap(a + i, n_attn), chip * CORES + other)
        for i in range(1, n_attn)
        for other in range(CORES)
    ]
    for device in known:
        pl.semaphore_signal(barrier, inc=1, device_id=device, device_id_type=MESH)

    load_q.wait()
    load_len.wait()
    pairs = (heads * req, heads * req)
    first = lax.broadcasted_iota(jnp.int32, pairs, 0)
    second = lax.broadcasted_iota(jnp.int32, pairs, 1)
    by_request = (lax.div(first, heads) == lax.rem(second, req)) & (
        lax.rem(first, heads) == lax.div(second, req)
    )
    stacked = jnp.concatenate([q_in[:, h * HD : (h + 1) * HD] for h in range(heads)], axis=0)
    q_rows[...] = dot(by_request.astype(F32).astype(BF16), stacked).astype(BF16)
    span = k_buf.shape[1]
    position = lax.broadcasted_iota(jnp.int32, (heads, span), 1)

    def score(g):
        load_k(g).wait()
        return [
            dot_nt(q_rows[i * heads : (i + 1) * heads, :], k_buf[i])
            for i in range(g * group, (g + 1) * group)
        ]

    def along_x(part, item_z, item_x, d, sem):
        item = att.at[part, item_z, item_x, pl.ds(0, couples + 1 - part)]
        return pltpu.make_async_remote_copy(
            src_ref=item,
            dst_ref=item,
            send_sem=sem,
            recv_sem=att_recv.at[part, item_z, item_x],
            device_id=(a, (z * n_x + wrap(x + d, n_x)) * CORES + core),
            device_id_type=MESH,
        )

    def along_z(part, item_z, item_x, d, sem):
        item = att.at[part, item_z, item_x, pl.ds(0, couples + 1 - part)]
        return pltpu.make_async_remote_copy(
            src_ref=item,
            dst_ref=item,
            send_sem=sem,
            recv_sem=att_recv.at[part, item_z, item_x],
            device_id=(a, (wrap(z + d, n_z) * n_x + x) * CORES + core),
            device_id_type=MESH,
        )

    def att_arrived(part, item_z, item_x):
        item = att.at[part, item_z, item_x, pl.ds(0, couples + 1 - part)]
        pltpu.make_async_copy(item, item, att_recv.at[part, item_z, item_x]).wait()

    sent = []
    mesh_pairs = (heads * part_req, heads * part_req)
    to_row = lax.broadcasted_iota(jnp.int32, mesh_pairs, 0)
    from_row = lax.broadcasted_iota(jnp.int32, mesh_pairs, 1)
    by_head = (
        (lax.div(from_row, heads) == lax.rem(to_row, part_req))
        & (lax.rem(from_row, heads) == lax.div(to_row, part_req))
    ).astype(F32).astype(BF16)

    def leave(part):
        span = heads * part_req
        own = dot(by_head, o_rows[part * span : (part + 1) * span, :]).astype(BF16)
        att[part, z, x, :couples] = own.reshape(couples, 2 * part_req, HD)
        if part == 0:
            load_gain.wait()
            place = lax.broadcasted_iota(jnp.int32, (2 * part_req, HD), 0)
            rest = gain_buf[...]
            tile = jnp.zeros((2 * part_req, HD), F32)
            for k in range(PARTS):
                piece = rest.astype(BF16).astype(F32)
                tile = tile + jnp.where(place == k, piece, 0.0)
                rest = rest - piece
            att[0, z, x, couples] = tile.astype(BF16)
            pl.semaphore_wait(barrier, len(known))
        steps = [(along_x, n_x), (along_z, n_z)]
        if part == 1:
            steps = steps[::-1]
        for k, (along, size) in enumerate(steps):
            for m, d in enumerate(ring(size)):
                copy = along(part, z, x, d, own_send.at[part, k, m])
                copy.start()
                sent.append(copy)

    ahead = score(0)
    for g in range(n_group):
        scores = ahead
        if g + 1 < n_group:
            ahead = score(g + 1)
        weights = []
        for j in range(group):
            masked = jnp.where(
                position < len_buf[g * group + j], scores[j] * (1.0 / math.sqrt(HD)), -1e30
            )
            expo = jnp.exp(masked - jnp.max(masked, axis=1, keepdims=True))
            weights.append((expo / jnp.sum(expo, axis=1, keepdims=True)).astype(BF16))
        load_v(g).wait()
        results = [dot(weights[j], v_buf[g * group + j]).astype(BF16) for j in range(group)]
        o_rows[g * group * heads : (g + 1) * group * heads, :] = jnp.concatenate(results, axis=0)
        if (g + 1) % (n_group // 2) == 0:
            leave(2 * g // n_group)

    def push_w(q):
        return pltpu.make_async_remote_copy(
            src_ref=out_weight.at[:, q],
            dst_ref=w_buf.at[q, core],
            send_sem=w_send.at[q],
            recv_sem=w_recv.at[q],
            device_id=(a, sibling),
            device_id_type=MESH,
        )

    for q in range(2):
        push_w(q).start()

    for k in range(max(n_x, n_z) - 1):
        if k < n_x - 1:
            from_x = wrap(x + ring(n_x)[k], n_x)
            att_arrived(0, z, from_x)
            for m, d in enumerate(ring(n_z)):
                copy = along_z(0, z, from_x, d, pass_send.at[0, k, m])
                copy.start()
                sent.append(copy)
        if k < n_z - 1:
            from_z = wrap(z + ring(n_z)[k], n_z)
            att_arrived(1, from_z, x)
            for m, d in enumerate(ring(n_x)):
                copy = along_x(1, from_z, x, d, pass_send.at[1, k, m])
                copy.start()
                sent.append(copy)

    depth = per_z * HD

    def load_gate_up(g):
        part = pl.ds(pl.multiple_of(g * depth, depth), depth)
        return pltpu.make_async_copy(
            gate_up.at[0, part, :], gate_up_buf.at[part, :], gate_sem.at[g]
        )

    load_down = pltpu.make_async_copy(down.at[0], down_buf, in_sem.at[5])
    for g in range(n_z):
        load_gate_up(g).start()
    load_down.start()

    load_ids.wait()
    load_gates.wait()
    earlier = (
        lax.broadcasted_iota(jnp.int32, (block, block), 0)
        < lax.broadcasted_iota(jnp.int32, (block, block), 1)
    ).astype(F32).astype(BF16)
    spread_row = lax.broadcasted_iota(jnp.int32, (slots, n_exp), 0)
    spread_col = lax.broadcasted_iota(jnp.int32, (slots, n_exp), 1)
    spread = (
        ((spread_row >= spread_col * CAP) & (spread_row < (spread_col + 1) * CAP))
        .astype(F32)
        .astype(BF16)
    )
    slot = lax.rem(lax.broadcasted_iota(jnp.int32, (slots, block), 0), CAP).astype(F32)
    local = lax.broadcasted_iota(jnp.int32, (n_exp, block), 0)
    for p in range(n_z):
        named = lax.div(local, per_z) * n_exp + p * per_z + lax.rem(local, per_z)
        chosen = jnp.zeros((n_exp, block), F32)
        weight = jnp.zeros((n_exp, block), F32)
        for k in range(ids_buf.shape[0]):
            hit = ids_buf[k : k + 1, :] == named
            chosen = chosen + jnp.where(hit, 1.0, 0.0)
            weight = weight + jnp.where(hit, gates_buf[k : k + 1, :], 0.0)
        rank = dot(chosen.astype(BF16), earlier)
        high = weight.astype(BF16)
        low = (weight - high.astype(F32)).astype(BF16)
        table = jnp.concatenate([rank.astype(BF16), chosen.astype(BF16), high, low], axis=1)
        wide = dot(spread, table)
        here = wide[:, :block] == slot
        select[p] = jnp.where(here, wide[:, block : 2 * block], 0.0).astype(BF16)
        comb_high[p] = jnp.where(here, wide[:, 2 * block : 3 * block], 0.0).T.astype(BF16)
        comb_low[p] = jnp.where(here, wide[:, 3 * block :], 0.0).T.astype(BF16)

    for q in range(2):
        load_w(q).wait()
        push_w(q).wait_recv()
    right = jnp.concatenate(
        [
            w_buf[q, other].reshape(couples * HD, HD)
            for q in range(2)
            for other in range(CORES)
        ],
        axis=1,
    )

    def push_part(b, other):
        return pltpu.make_async_remote_copy(
            src_ref=part_send.at[b, other],
            dst_ref=part_recv.at[a, core],
            send_sem=rs_send.at[b * CORES + other],
            recv_sem=rs_recv.at[a * CORES + core],
            device_id=(b, chip * CORES + other),
            device_id_type=MESH,
        )

    for i in [0, *ring(n_z)]:
        b = wrap(z + i, n_z)
        for d in ring(n_x):
            if i > 0:
                att_arrived(0, b, wrap(x + d, n_x))
            att_arrived(1, b, wrap(x + d, n_x))
        if i > 0:
            att_arrived(0, b, x)
        left = jnp.concatenate(
            [att[:, b, :, k].reshape(2 * half, HD) for k in range(couples)], axis=1
        )
        wide = dot(left, right)
        pieces = []
        for xx in range(n_x):
            for part in range(2):
                top = (part * n_x + xx) * 2 * part_req
                pieces.append(
                    wide[top : top + part_req, : CORES * HD]
                    + wide[top + part_req : top + 2 * part_req, CORES * HD :]
                )
        product = jnp.concatenate(pieces, axis=0)
        for other in range(CORES):
            part_send[b, other] = product[:, other * HD : (other + 1) * HD].astype(BF16)

        @pl.when(b != a)
        def _():
            for other in range(CORES):
                push_part(b, other).start()

        @pl.when(b == a)
        def _():
            push_part(b, 1 - core).start()
            part_recv[a, core] = part_send[b, core]

    for k in range(n_z * n_x):
        tile = att[0, k // n_x, k % n_x, couples].astype(F32)
        gain_inv[core, k] = 1.0 / jnp.sum(tile[:PARTS], axis=0, keepdims=True)
    push_gain = pltpu.make_async_remote_copy(
        src_ref=gain_inv.at[core],
        dst_ref=gain_inv.at[core],
        send_sem=gain_send,
        recv_sem=gain_recv,
        device_id=(a, sibling),
        device_id_type=MESH,
    )
    push_gain.start()

    for i in range(n_attn):
        b = wrap(a + i, n_attn)
        for other in range(CORES):
            def arrived(b=b, other=other):
                pltpu.make_async_copy(
                    part_recv.at[b, other],
                    part_recv.at[b, other],
                    rs_recv.at[b * CORES + other],
                ).wait()

            if i > 0:
                arrived()
            else:
                pl.when(core != other)(arrived)

    load_res.wait()
    totals = []
    for other in range(CORES):
        total = part_recv[0, other].astype(F32)
        for b in range(1, n_attn):
            total = total + part_recv[b, other].astype(F32)
        totals.append(total)
    state = res_buf[...] + jnp.concatenate(
        [totals[other][xx * req : (xx + 1) * req] for xx in range(n_x) for other in range(CORES)],
        axis=0,
    )
    out[...] = state
    scaled = (state * gain_buf[...]).astype(BF16)

    def push_x(zz, to_a, to_lane):
        return pltpu.make_async_remote_copy(
            src_ref=x_send.at[(zz * n_attn + to_a) * per_z + to_lane],
            dst_ref=x_recv.at[e, a],
            send_sem=xs_sem,
            recv_sem=xr_sem.at[z],
            device_id=(to_a, zz * per_z + to_lane),
            device_id_type=MESH,
        )

    around = [*range(1, n_attn), 0]
    for dz in far:
        zz = wrap(z + dz, n_z)
        picked = dot(select[zz], scaled).astype(BF16)
        x_send[pl.ds(zz * n_exp, n_exp)] = picked.reshape(n_exp, CAP, HD)

        def start_x(k, carry, zz=zz, dz=dz):
            to = wrap(lane + per_z // 2 + k, per_z)
            for i in around:
                copy = push_x(zz, wrap(a + i, n_attn), to)
                if dz == 0 and i == 0:
                    pl.when(to != lane)(copy.start)
                else:
                    copy.start()
            return carry

        lax.fori_loop(0, per_z, start_x, 0)
    own_x = pltpu.make_async_copy(
        x_send.at[(z * n_attn + a) * per_z + lane], x_recv.at[e, a], xr_sem.at[z]
    )
    own_x.start()

    squares = jnp.zeros((rows, HD), F32)
    push_gain.wait_recv()
    for step, dz in enumerate(far):
        zz = wrap(z + n_z - dz, n_z)
        arrived = x_recv.at[pl.ds(zz * per_z, per_z)]
        pltpu.make_async_copy(arrived, arrived, xr_sem.at[zz]).wait()
        load_gate_up(zz).wait()
        pieces = [x_recv[zz * per_z + q].reshape(rows, HD) for q in range(per_z)]
        for q in range(per_z):
            plain = pieces[q].astype(F32) * gain_inv[q % CORES, zz * n_x + q // CORES]
            squares = squares + plain * plain
        left = jnp.concatenate(pieces, axis=1)
        product = dot(left, gate_up_buf[pl.ds(pl.multiple_of(zz * depth, depth), depth), :])
        if step == 0:
            mixed[...] = product
        else:
            mixed[...] += product

    scale = lax.rsqrt(jnp.sum(squares, axis=1, keepdims=True) / features + 1e-06)
    gate = mixed[:, :width] * scale
    up = mixed[:, width:] * scale
    inner = (gate / (1.0 + jnp.exp(-gate)) * up).astype(BF16)

    load_down.wait()

    def push_y(to_a, to_e):
        return pltpu.make_async_remote_copy(
            src_ref=y_send.at[to_e * n_attn + to_a],
            dst_ref=y_recv.at[(z * n_attn + a) * per_z + lane],
            send_sem=ys_sem,
            recv_sem=yr_sem.at[z],
            device_id=(to_a, to_e),
            device_id_type=MESH,
        )

    for dz in far:
        zz = wrap(z + dz, n_z)
        produced = dot(
            inner, down_buf[:, pl.ds(pl.multiple_of(zz * depth, depth), depth)]
        ).astype(BF16)
        for q in range(per_z):
            y_send[pl.ds((zz * per_z + q) * n_attn, n_attn)] = produced[
                :, q * HD : (q + 1) * HD
            ].reshape(n_attn, CAP, HD)

        def start_y(k, carry, zz=zz, dz=dz):
            to = wrap(lane + per_z // 2 + k, per_z)
            for i in around:
                copy = push_y(wrap(a + i, n_attn), zz * per_z + to)
                if dz == 0 and i == 0:
                    pl.when(to != lane)(copy.start)
                else:
                    copy.start()
            return carry

        lax.fori_loop(0, per_z, start_y, 0)
    own_y = pltpu.make_async_copy(
        y_send.at[e * n_attn + a], y_recv.at[(z * n_attn + a) * per_z + lane], yr_sem.at[z]
    )
    own_y.start()

    for dz in far:
        p = wrap(z + n_z - dz, n_z)
        arrived = y_recv.at[pl.ds(p * n_exp, n_exp)]
        pltpu.make_async_copy(arrived, arrived, yr_sem.at[p]).wait()
        back = y_recv[pl.ds(p * n_exp, n_exp)].reshape(slots, HD)
        out[...] += dot(comb_high[p], back) + dot(comb_low[p], back)

    for copy in sent:
        copy.wait_send()
    for q in range(2):
        push_w(q).wait_send()
    push_gain.wait_send()
    for b in range(n_attn):
        for other in range(CORES):
            def left_here(b=b, other=other):
                push_part(b, other).wait_send()

            pl.when(jnp.logical_not((b == a) & (core == other)))(left_here)
    for buffer, sem in ((x_send, xs_sem), (y_send, ys_sem)):
        gone = buffer.at[pl.ds(0, experts - 1)]
        pltpu.make_async_copy(gone, gone, sem).wait()


def body(
    n_attn,
    n_exp,
    residual,
    queries,
    keys,
    values,
    lengths,
    out_weight,
    norm_gain,
    expert_ids,
    gates,
    gate_up,
    down,
):
    req, span = keys.shape[0], keys.shape[1]
    heads = queries.shape[1] // HD
    width = down.shape[1]
    features = gate_up.shape[1]
    block = residual.shape[0]
    n_z = n_attn
    n_x = n_exp // (CORES * n_z)
    rows = n_attn * CAP
    slots = n_exp * CAP
    half = n_x * req
    groups = 4
    top = expert_ids.shape[1]
    cfg = (n_attn, n_z, n_x, req, heads, width)
    anywhere = pl.BlockSpec(memory_space=pl.ANY)
    vmem = pltpu.VMEM
    sem = pltpu.SemaphoreType.DMA
    return pl.pallas_call(
        functools.partial(layer_kernel, cfg),
        out_shape=jax.ShapeDtypeStruct(residual.shape, F32),
        in_specs=[anywhere] * 11,
        out_specs=pl.BlockSpec(memory_space=pltpu.VMEM),
        scratch_shapes=[
            vmem(queries.shape, BF16),
            vmem((req * heads, HD), BF16),
            vmem((req * heads, HD), BF16),
            vmem(keys.shape, BF16),
            vmem(values.shape, BF16),
            vmem((2, CORES, heads // 2, HD, HD), BF16),
            vmem(residual.shape, F32),
            pltpu.SMEM(lengths.shape, jnp.int32),
            vmem((1, HD), F32),
            vmem((CORES, n_z * n_x, 1, HD), F32),
            vmem((top, block), jnp.int32),
            vmem((top, block), F32),
            vmem((2, n_z, n_x, heads // 2 + 1, req, HD), BF16),
            vmem((n_attn, CORES, half, HD), BF16),
            vmem((n_attn, CORES, half, HD), BF16),
            vmem((n_attn, slots, block), BF16),
            vmem((n_attn, block, slots), BF16),
            vmem((n_attn, block, slots), BF16),
            vmem((n_attn * n_exp, CAP, HD), BF16),
            vmem((n_exp, n_attn, CAP, HD), BF16),
            vmem((features, 2 * width), BF16),
            vmem((width, features), BF16),
            vmem((rows, 2 * width), F32),
            vmem((n_exp * n_attn, CAP, HD), BF16),
            vmem((n_attn * n_exp, CAP, HD), BF16),
            sem((9,)),
            sem((groups,)),
            sem((groups,)),
            sem((n_z,)),
            sem((2,)),
            sem((2,)),
            sem,
            sem,
            sem((2, 2, max(n_x, n_z) - 1)),
            sem((2, max(n_x, n_z) - 1, max(n_x, n_z) - 1)),
            sem((2, n_z, n_x)),
            sem((n_attn * CORES,)),
            sem((n_attn * CORES,)),
            sem,
            sem((n_z,)),
            sem,
            sem((n_attn,)),
        ],
        compiler_params=pltpu.CompilerParams(
            collective_id=0, has_side_effects=True, vmem_limit_bytes=58 * 1024 * 1024
        ),
        name="layer",
    )(
        lengths,
        residual,
        queries,
        keys,
        values,
        out_weight.reshape(heads // 2, 2, HD, HD),
        norm_gain.reshape(1, HD),
        expert_ids.T,
        gates.T,
        gate_up,
        down,
    )


def solution(mesh):
    in_specs = (
        P("attn", "expert"),
        P("expert", "attn"),
        P("expert", None, "attn"),
        P("expert", None, "attn"),
        P("expert"),
        P("attn", "expert"),
        P("expert"),
        P("attn", None),
        P("attn", None),
        P(("attn", "expert"), None, None),
        P(("attn", "expert"), None, None),
    )
    run = functools.partial(body, mesh.shape["attn"], mesh.shape["expert"])
    return jax.shard_map(
        run, mesh=mesh, in_specs=in_specs, out_specs=P("attn", "expert"), check_vma=False
    )
```

time: 50.9 us -> 48.8 us (0.959)
  Pallas kernels: 49.2 us -> 47.2 us
    pallas_call x1, Pallas kernels: 49.2 us -> 47.2 us  [body(): pl.pallas_call(functools.partial(layer_kernel, cfg), out_shape=jax.ShapeD...]
where the time goes in v3:
time: 48.8 us; the launch traced here: 48.7 us
  Pallas kernels  47.2 us (97%)
  local copies, waits for them, and re-layouts  1.47 us (3%)
    pallas_call x1, Pallas kernels, body(): pl.pallas_call(functools.partial(layer_kernel, cfg), out_shape=jax.ShapeD...  47.2 us
    unnamed x1, local copies, waits for them, and re-layouts  1.47 us

profile of v3, /device:TPU:1, one launch (start us, length us, event | category | flops | bytes accessed | tf_op | source)
XLA Modules:
  0.0 48.7 jit_solution(14327051092932972547)
XLA Ops:
  0.0 47.2 %layer.1 = f32[128,128]{1,0:T(8,128)} custom-call(s32[16]{0:T(128)} %lengths.1, f32[128,128]{1,0:T(8,128)} %residual.1, bf16[16,2048]{1,0:T(8,128)(2,1)} %queries.1, bf16[16,1024,128]{2,1,0:T(8,128)(2,1)} %keys.1, bf16[16,1024,128]{2,1,0:T(8,128)(2,1)} %values.1, bf16[8,2,128,128]{3,2,1,0:T(8,128)(2,1)} %bitcast.4, f32[1,128]{1,0:T(1,128)} %bitcast.7, ...), custom_call_target="tpu_custom_call" | custom-call | tf_op jit(solution)/shard_map/layer/pallas_call | solution.py:571
  47.2 1.5 %copy.13 = f32[128,128]{1,0:T(8,128)} copy(f32[128,128]{1,0:T(8,128)} %layer.1) | data formatting | bytes 131072

commit v4 on v3

--- a/solution.py
+++ b/solution.py
@@ -90,10 +90,10 @@
     half = n_x * req
     features = n_exp * HD
     slots = n_exp * CAP
-    rows = n_attn * CAP
     experts = n_attn * n_exp
     part_req = req // 2
     couples = heads // 2
+    places = n_attn // 2
     far = [n_z // 2, *(d for d in range(1, n_z) if d != n_z // 2), 0]
     a = lax.axis_index("attn")
     e = lax.axis_index("expert")
@@ -171,31 +171,57 @@
             for i in range(g * group, (g + 1) * group)
         ]
 
-    def along_x(part, item_z, item_x, d, sem):
-        item = att.at[part, item_z, item_x, pl.ds(0, couples + 1 - part)]
+    def quarter(part, side, item_z, item_x):
+        count = couples // 2
+        extra = 1 if part == 0 and side == 1 else 0
+        return att.at[part, item_z, item_x, pl.ds(side * count, count + extra)]
+
+    def along(axis, part, side, item_z, item_x, d, sem):
+        item = quarter(part, side, item_z, item_x)
+        if axis == 0:
+            to = z * n_x + wrap(x + d, n_x)
+        else:
+            to = wrap(z + d, n_z) * n_x + x
         return pltpu.make_async_remote_copy(
             src_ref=item,
             dst_ref=item,
             send_sem=sem,
-            recv_sem=att_recv.at[part, item_z, item_x],
-            device_id=(a, (z * n_x + wrap(x + d, n_x)) * CORES + core),
+            recv_sem=att_recv.at[part, side, item_z, item_x],
+            device_id=(a, to * CORES + core),
             device_id_type=MESH,
         )
 
-    def along_z(part, item_z, item_x, d, sem):
-        item = att.at[part, item_z, item_x, pl.ds(0, couples + 1 - part)]
-        return pltpu.make_async_remote_copy(
-            src_ref=item,
-            dst_ref=item,
-            send_sem=sem,
-            recv_sem=att_recv.at[part, item_z, item_x],
-            device_id=(a, (wrap(z + d, n_z) * n_x + x) * CORES + core),
-            device_id_type=MESH,
-        )
-
-    def att_arrived(part, item_z, item_x):
-        item = att.at[part, item_z, item_x, pl.ds(0, couples + 1 - part)]
-        pltpu.make_async_copy(item, item, att_recv.at[part, item_z, item_x]).wait()
+    def att_arrived(part, side, item_z, item_x):
+        item = quarter(part, side, item_z, item_x)
+        pltpu.make_async_copy(item, item, att_recv.at[part, side, item_z, item_x]).wait()
+
+    rings = (ring(n_x), ring(n_z))
+
+    def own_away(part, second):
+        for k in range(max(n_x, n_z) - 1):
+            for side in range(2):
+                axis = 1 - side if second else side
+                if k < len(rings[axis]):
+                    copy = along(
+                        axis, part, side, z, x, rings[axis][k], own_send.at[part, side, axis, k]
+                    )
+                    copy.start()
+                    sent.append(copy)
+
+    def pass_on(part):
+        for k in range(max(n_x, n_z) - 1):
+            for side in range(2):
+                if k < len(rings[side]):
+                    d = rings[side][k]
+                    from_z = wrap(z + d, n_z) if side else z
+                    from_x = x if side else wrap(x + d, n_x)
+                    att_arrived(part, side, from_z, from_x)
+                    for m, onward in enumerate(rings[1 - side]):
+                        copy = along(
+                            1 - side, part, side, from_z, from_x, onward, pass_send.at[part, side, k, m]
+                        )
+                        copy.start()
+                        sent.append(copy)
 
     sent = []
     mesh_pairs = (heads * part_req, heads * part_req)
@@ -221,14 +247,10 @@
                 rest = rest - piece
             att[0, z, x, couples] = tile.astype(BF16)
             pl.semaphore_wait(barrier, len(known))
-        steps = [(along_x, n_x), (along_z, n_z)]
+        own_away(part, False)
         if part == 1:
-            steps = steps[::-1]
-        for k, (along, size) in enumerate(steps):
-            for m, d in enumerate(ring(size)):
-                copy = along(part, z, x, d, own_send.at[part, k, m])
-                copy.start()
-                sent.append(copy)
+            pass_on(0)
+        own_away(part, True)
 
     ahead = score(0)
     for g in range(n_group):
@@ -261,21 +283,7 @@
     for q in range(2):
         push_w(q).start()
 
-    for k in range(max(n_x, n_z) - 1):
-        if k < n_x - 1:
-            from_x = wrap(x + ring(n_x)[k], n_x)
-            att_arrived(0, z, from_x)
-            for m, d in enumerate(ring(n_z)):
-                copy = along_z(0, z, from_x, d, pass_send.at[0, k, m])
-                copy.start()
-                sent.append(copy)
-        if k < n_z - 1:
-            from_z = wrap(z + ring(n_z)[k], n_z)
-            att_arrived(1, from_z, x)
-            for m, d in enumerate(ring(n_x)):
-                copy = along_x(1, from_z, x, d, pass_send.at[1, k, m])
-                copy.start()
-                sent.append(copy)
+    pass_on(1)
 
     depth = per_z * HD
 
@@ -305,8 +313,11 @@
     )
     slot = lax.rem(lax.broadcasted_iota(jnp.int32, (slots, block), 0), CAP).astype(F32)
     local = lax.broadcasted_iota(jnp.int32, (n_exp, block), 0)
+    turn = lax.div(local, per_z)
+    turn = lax.div(turn, places) + 2 * lax.rem(turn, places)
+    first_named = lax.rem(a + turn, n_attn) * n_exp + lax.rem(local, per_z)
     for p in range(n_z):
-        named = lax.div(local, per_z) * n_exp + p * per_z + lax.rem(local, per_z)
+        named = first_named + p * per_z
         chosen = jnp.zeros((n_exp, block), F32)
         weight = jnp.zeros((n_exp, block), F32)
         for k in range(ids_buf.shape[0]):
@@ -347,12 +358,12 @@
 
     for i in [0, *ring(n_z)]:
         b = wrap(z + i, n_z)
-        for d in ring(n_x):
+        for part in range(2):
+            for d in ring(n_x):
+                att_arrived(part, 1, b, wrap(x + d, n_x))
             if i > 0:
-                att_arrived(0, b, wrap(x + d, n_x))
-            att_arrived(1, b, wrap(x + d, n_x))
-        if i > 0:
-            att_arrived(0, b, x)
+                for d in [0, *ring(n_x)]:
+                    att_arrived(part, 0, b, wrap(x + d, n_x))
         left = jnp.concatenate(
             [att[:, b, :, k].reshape(2 * half, HD) for k in range(couples)], axis=1
         )
@@ -421,105 +432,111 @@
     out[...] = state
     scaled = (state * gain_buf[...]).astype(BF16)
 
-    def push_x(zz, to_a, to_lane):
+    def spot(zz, even, place, to_lane):
+        return ((zz * 2 + even) * places + place) * per_z + to_lane
+
+    def back_place(even, place):
+        return (n_attn - even - 2 * place) % n_attn // 2
+
+    def push_x(even, place, zz, to_lane):
         return pltpu.make_async_remote_copy(
-            src_ref=x_send.at[(zz * n_attn + to_a) * per_z + to_lane],
-            dst_ref=x_recv.at[e, a],
+            src_ref=x_send.at[spot(zz, even, place, to_lane)],
+            dst_ref=x_recv.at[even, e, back_place(even, place)],
             send_sem=xs_sem,
-            recv_sem=xr_sem.at[z],
-            device_id=(to_a, zz * per_z + to_lane),
+            recv_sem=xr_sem.at[even, z],
+            device_id=(wrap(a + even + 2 * place, n_attn), zz * per_z + to_lane),
             device_id_type=MESH,
         )
 
-    around = [*range(1, n_attn), 0]
+    def spread_out(push, even, dz):
+        zz = wrap(z + dz, n_z)
+
+        def step(k, carry):
+            to = wrap(lane + per_z // 2 + k, per_z)
+            for place in reversed(range(places)):
+                copy = push(even, place, zz, to)
+                if dz == 0 and even == 0 and place == 0:
+                    pl.when(to != lane)(copy.start)
+                else:
+                    copy.start()
+            return carry
+
+        lax.fori_loop(0, per_z, step, 0)
+
     for dz in far:
         zz = wrap(z + dz, n_z)
         picked = dot(select[zz], scaled).astype(BF16)
         x_send[pl.ds(zz * n_exp, n_exp)] = picked.reshape(n_exp, CAP, HD)
-
-        def start_x(k, carry, zz=zz, dz=dz):
-            to = wrap(lane + per_z // 2 + k, per_z)
-            for i in around:
-                copy = push_x(zz, wrap(a + i, n_attn), to)
-                if dz == 0 and i == 0:
-                    pl.when(to != lane)(copy.start)
-                else:
-                    copy.start()
-            return carry
-
-        lax.fori_loop(0, per_z, start_x, 0)
+        spread_out(push_x, 0, dz)
     own_x = pltpu.make_async_copy(
-        x_send.at[(z * n_attn + a) * per_z + lane], x_recv.at[e, a], xr_sem.at[z]
+        x_send.at[spot(z, 0, 0, lane)], x_recv.at[0, e, 0], xr_sem.at[0, z]
     )
     own_x.start()
-
-    squares = jnp.zeros((rows, HD), F32)
-    push_gain.wait_recv()
-    for step, dz in enumerate(far):
-        zz = wrap(z + n_z - dz, n_z)
-        arrived = x_recv.at[pl.ds(zz * per_z, per_z)]
-        pltpu.make_async_copy(arrived, arrived, xr_sem.at[zz]).wait()
-        load_gate_up(zz).wait()
-        pieces = [x_recv[zz * per_z + q].reshape(rows, HD) for q in range(per_z)]
-        for q in range(per_z):
-            plain = pieces[q].astype(F32) * gain_inv[q % CORES, zz * n_x + q // CORES]
-            squares = squares + plain * plain
-        left = jnp.concatenate(pieces, axis=1)
-        product = dot(left, gate_up_buf[pl.ds(pl.multiple_of(zz * depth, depth), depth), :])
-        if step == 0:
-            mixed[...] = product
-        else:
-            mixed[...] += product
-
-    scale = lax.rsqrt(jnp.sum(squares, axis=1, keepdims=True) / features + 1e-06)
-    gate = mixed[:, :width] * scale
-    up = mixed[:, width:] * scale
-    inner = (gate / (1.0 + jnp.exp(-gate)) * up).astype(BF16)
-
-    load_down.wait()
-
-    def push_y(to_a, to_e):
+    for dz in far:
+        spread_out(push_x, 1, dz)
+
+    def push_y(even, place, zz, to_lane):
         return pltpu.make_async_remote_copy(
-            src_ref=y_send.at[to_e * n_attn + to_a],
-            dst_ref=y_recv.at[(z * n_attn + a) * per_z + lane],
+            src_ref=y_send.at[zz * per_z + to_lane, even, place],
+            dst_ref=y_recv.at[even, z, back_place(even, place), lane],
             send_sem=ys_sem,
-            recv_sem=yr_sem.at[z],
-            device_id=(to_a, to_e),
+            recv_sem=yr_sem.at[even, z],
+            device_id=(wrap(a + even + 2 * place, n_attn), zz * per_z + to_lane),
             device_id_type=MESH,
         )
 
-    for dz in far:
-        zz = wrap(z + dz, n_z)
-        produced = dot(
-            inner, down_buf[:, pl.ds(pl.multiple_of(zz * depth, depth), depth)]
-        ).astype(BF16)
-        for q in range(per_z):
-            y_send[pl.ds((zz * per_z + q) * n_attn, n_attn)] = produced[
-                :, q * HD : (q + 1) * HD
-            ].reshape(n_attn, CAP, HD)
-
-        def start_y(k, carry, zz=zz, dz=dz):
-            to = wrap(lane + per_z // 2 + k, per_z)
-            for i in around:
-                copy = push_y(wrap(a + i, n_attn), zz * per_z + to)
-                if dz == 0 and i == 0:
-                    pl.when(to != lane)(copy.start)
-                else:
-                    copy.start()
-            return carry
-
-        lax.fori_loop(0, per_z, start_y, 0)
-    own_y = pltpu.make_async_copy(
-        y_send.at[e * n_attn + a], y_recv.at[(z * n_attn + a) * per_z + lane], yr_sem.at[z]
-    )
-    own_y.start()
-
-    for dz in far:
-        p = wrap(z + n_z - dz, n_z)
-        arrived = y_recv.at[pl.ds(p * n_exp, n_exp)]
-        pltpu.make_async_copy(arrived, arrived, yr_sem.at[p]).wait()
-        back = y_recv[pl.ds(p * n_exp, n_exp)].reshape(slots, HD)
-        out[...] += dot(comb_high[p], back) + dot(comb_low[p], back)
+    push_gain.wait_recv()
+    part_rows = places * CAP
+    for even in range(2):
+        squares = jnp.zeros((part_rows, HD), F32)
+        for step, dz in enumerate(far):
+            zz = wrap(z + n_z - dz, n_z)
+            arrived = x_recv.at[even, pl.ds(zz * per_z, per_z)]
+            pltpu.make_async_copy(arrived, arrived, xr_sem.at[even, zz]).wait()
+            if even == 0:
+                load_gate_up(zz).wait()
+            pieces = [x_recv[even, zz * per_z + q].reshape(part_rows, HD) for q in range(per_z)]
+            for q in range(per_z):
+                plain = pieces[q].astype(F32) * gain_inv[q % CORES, zz * n_x + q // CORES]
+                squares = squares + plain * plain
+            left = jnp.concatenate(pieces, axis=1)
+            product = dot(left, gate_up_buf[pl.ds(pl.multiple_of(zz * depth, depth), depth), :])
+            if step == 0:
+                mixed[...] = product
+            else:
+                mixed[...] += product
+        scale = lax.rsqrt(jnp.sum(squares, axis=1, keepdims=True) / features + 1e-06)
+        gate = mixed[:, :width] * scale
+        up = mixed[:, width:] * scale
+        inner = (gate / (1.0 + jnp.exp(-gate)) * up).astype(BF16)
+
+        if even == 0:
+            load_down.wait()
+        for dz in far:
+            zz = wrap(z + dz, n_z)
+            produced = dot(
+                inner, down_buf[:, pl.ds(pl.multiple_of(zz * depth, depth), depth)]
+            ).astype(BF16)
+            for q in range(per_z):
+                y_send[zz * per_z + q, even] = produced[:, q * HD : (q + 1) * HD].reshape(
+                    places, CAP, HD
+                )
+            spread_out(push_y, even, dz)
+        if even == 0:
+            own_y = pltpu.make_async_copy(
+                y_send.at[e, 0, 0], y_recv.at[0, z, 0, lane], yr_sem.at[0, z]
+            )
+            own_y.start()
+
+    part_slots = slots // 2
+    for even in range(2):
+        for dz in far:
+            zz = wrap(z + n_z - dz, n_z)
+            arrived = y_recv.at[even, zz]
+            pltpu.make_async_copy(arrived, arrived, yr_sem.at[even, zz]).wait()
+            back = y_recv[even, zz].reshape(part_slots, HD)
+            lanes = slice(even * part_slots, (even + 1) * part_slots)
+            out[...] += dot(comb_high[zz, :, lanes], back) + dot(comb_low[zz, :, lanes], back)
 
     for copy in sent:
         copy.wait_send()
@@ -532,8 +549,8 @@
                 push_part(b, other).wait_send()
 
             pl.when(jnp.logical_not((b == a) & (core == other)))(left_here)
-    for buffer, sem in ((x_send, xs_sem), (y_send, ys_sem)):
-        gone = buffer.at[pl.ds(0, experts - 1)]
+    for sem in (xs_sem, ys_sem):
+        gone = x_send.at[pl.ds(0, experts - 1)]
         pltpu.make_async_copy(gone, gone, sem).wait()
 
 
@@ -570,7 +587,7 @@
     sem = pltpu.SemaphoreType.DMA
     return pl.pallas_call(
         functools.partial(layer_kernel, cfg),
-        out_shape=jax.ShapeDtypeStruct(residual.shape, F32),
+        out_shape=pltpu.VMEM(residual.shape, F32),
         in_specs=[anywhere] * 11,
         out_specs=pl.BlockSpec(memory_space=pltpu.VMEM),
         scratch_shapes=[
@@ -593,12 +610,12 @@
             vmem((n_attn, block, slots), BF16),
             vmem((n_attn, block, slots), BF16),
             vmem((n_attn * n_exp, CAP, HD), BF16),
-            vmem((n_exp, n_attn, CAP, HD), BF16),
+            vmem((2, n_exp, n_attn // 2, CAP, HD), BF16),
             vmem((features, 2 * width), BF16),
             vmem((width, features), BF16),
-            vmem((rows, 2 * width), F32),
-            vmem((n_exp * n_attn, CAP, HD), BF16),
-            vmem((n_attn * n_exp, CAP, HD), BF16),
+            vmem((rows // 2, 2 * width), F32),
+            vmem((n_exp, 2, n_attn // 2, CAP, HD), BF16),
+            vmem((2, n_z, n_attn // 2, n_x * CORES, CAP, HD), BF16),
             sem((9,)),
             sem((groups,)),
             sem((groups,)),
@@ -607,15 +624,15 @@
             sem((2,)),
             sem,
             sem,
-            sem((2, 2, max(n_x, n_z) - 1)),
-            sem((2, max(n_x, n_z) - 1, max(n_x, n_z) - 1)),
-            sem((2, n_z, n_x)),
+            sem((2, 2, 2, max(n_x, n_z) - 1)),
+            sem((2, 2, max(n_x, n_z) - 1, max(n_x, n_z) - 1)),
+            sem((2, 2, n_z, n_x)),
             sem((n_attn * CORES,)),
             sem((n_attn * CORES,)),
             sem,
-            sem((n_z,)),
+            sem((2, n_z)),
             sem,
-            sem((n_attn,)),
+            sem((2, n_z)),
         ],
         compiler_params=pltpu.CompilerParams(
             collective_id=0, has_side_effects=True, vmem_limit_bytes=58 * 1024 * 1024

time: 48.8 us -> 46.1 us (0.945)
  Pallas kernels: 47.2 us -> 45.3 us
  local copies, waits for them, and re-layouts: 1.47 us -> 0.63 us
    pallas_call x1, Pallas kernels: 47.2 us -> 45.3 us  [body(): pl.pallas_call(functools.partial(layer_kernel, cfg), out_shape=pltpu.VMEM...]
    unnamed x1, local copies, waits for them, and re-layouts: 1.47 us -> 0.63 us
where the time goes in v4:
time: 46.1 us; the launch traced here: 46 us
  Pallas kernels  45.3 us (98%)
  local copies, waits for them, and re-layouts  0.63 us (1%)
    pallas_call x1, Pallas kernels, body(): pl.pallas_call(functools.partial(layer_kernel, cfg), out_shape=pltpu.VMEM...  45.3 us

profile of v4, /device:TPU:1, one launch (start us, length us, event | category | flops | bytes accessed | tf_op | source)
XLA Modules:
  0.0 46.0 jit_solution(17288530007738880247)
XLA Ops:
  0.0 45.3 %layer.1 = f32[128,128]{1,0:T(8,128)S(1)} custom-call(s32[16]{0:T(128)} %lengths.1, f32[128,128]{1,0:T(8,128)} %residual.1, bf16[16,2048]{1,0:T(8,128)(2,1)} %queries.1, bf16[16,1024,128]{2,1,0:T(8,128)(2,1)} %keys.1, bf16[16,1024,128]{2,1,0:T(8,128)(2,1)} %values.1, bf16[8,2,128,128]{3,2,1,0:T(8,128)(2,1)} %bitcast.4, f32[1,128]{1,0:T(1,128)} %bitcast.7, ...), custom_call_target="tpu_custom_call" | custom-call | tf_op jit(solution)/shard_map/layer/pallas_call | solution.py:588
  45.3 0.6 %copy.13 = f32[128,128]{1,0:T(8,128)} copy(f32[128,128]{1,0:T(8,128)S(1)} %layer.1) | data formatting | bytes 131072

commit v5 on v3

--- a/solution.py
+++ b/solution.py
@@ -171,31 +171,57 @@
             for i in range(g * group, (g + 1) * group)
         ]
 
-    def along_x(part, item_z, item_x, d, sem):
-        item = att.at[part, item_z, item_x, pl.ds(0, couples + 1 - part)]
+    def quarter(part, side, item_z, item_x):
+        count = couples // 2
+        extra = 1 if part == 0 and side == 1 else 0
+        return att.at[part, item_z, item_x, pl.ds(side * count, count + extra)]
+
+    def along(axis, part, side, item_z, item_x, d, sem):
+        item = quarter(part, side, item_z, item_x)
+        if axis == 0:
+            to = z * n_x + wrap(x + d, n_x)
+        else:
+            to = wrap(z + d, n_z) * n_x + x
         return pltpu.make_async_remote_copy(
             src_ref=item,
             dst_ref=item,
             send_sem=sem,
-            recv_sem=att_recv.at[part, item_z, item_x],
-            device_id=(a, (z * n_x + wrap(x + d, n_x)) * CORES + core),
+            recv_sem=att_recv.at[part, side, item_z, item_x],
+            device_id=(a, to * CORES + core),
             device_id_type=MESH,
         )
 
-    def along_z(part, item_z, item_x, d, sem):
-        item = att.at[part, item_z, item_x, pl.ds(0, couples + 1 - part)]
-        return pltpu.make_async_remote_copy(
-            src_ref=item,
-            dst_ref=item,
-            send_sem=sem,
-            recv_sem=att_recv.at[part, item_z, item_x],
-            device_id=(a, (wrap(z + d, n_z) * n_x + x) * CORES + core),
-            device_id_type=MESH,
-        )
-
-    def att_arrived(part, item_z, item_x):
-        item = att.at[part, item_z, item_x, pl.ds(0, couples + 1 - part)]
-        pltpu.make_async_copy(item, item, att_recv.at[part, item_z, item_x]).wait()
+    def att_arrived(part, side, item_z, item_x):
+        item = quarter(part, side, item_z, item_x)
+        pltpu.make_async_copy(item, item, att_recv.at[part, side, item_z, item_x]).wait()
+
+    rings = (ring(n_x), ring(n_z))
+
+    def own_away(part, second):
+        for k in range(max(n_x, n_z) - 1):
+            for side in range(2):
+                axis = 1 - side if second else side
+                if k < len(rings[axis]):
+                    copy = along(
+                        axis, part, side, z, x, rings[axis][k], own_send.at[part, side, axis, k]
+                    )
+                    copy.start()
+                    sent.append(copy)
+
+    def pass_on(part):
+        for k in range(max(n_x, n_z) - 1):
+            for side in range(2):
+                if k < len(rings[side]):
+                    d = rings[side][k]
+                    from_z = wrap(z + d, n_z) if side else z
+                    from_x = x if side else wrap(x + d, n_x)
+                    att_arrived(part, side, from_z, from_x)
+                    for m, onward in enumerate(rings[1 - side]):
+                        copy = along(
+                            1 - side, part, side, from_z, from_x, onward, pass_send.at[part, side, k, m]
+                        )
+                        copy.start()
+                        sent.append(copy)
 
     sent = []
     mesh_pairs = (heads * part_req, heads * part_req)
@@ -221,14 +247,10 @@
                 rest = rest - piece
             att[0, z, x, couples] = tile.astype(BF16)
             pl.semaphore_wait(barrier, len(known))
-        steps = [(along_x, n_x), (along_z, n_z)]
+        own_away(part, False)
         if part == 1:
-            steps = steps[::-1]
-        for k, (along, size) in enumerate(steps):
-            for m, d in enumerate(ring(size)):
-                copy = along(part, z, x, d, own_send.at[part, k, m])
-                copy.start()
-                sent.append(copy)
+            pass_on(0)
+        own_away(part, True)
 
     ahead = score(0)
     for g in range(n_group):
@@ -261,21 +283,7 @@
     for q in range(2):
         push_w(q).start()
 
-    for k in range(max(n_x, n_z) - 1):
-        if k < n_x - 1:
-            from_x = wrap(x + ring(n_x)[k], n_x)
-            att_arrived(0, z, from_x)
-            for m, d in enumerate(ring(n_z)):
-                copy = along_z(0, z, from_x, d, pass_send.at[0, k, m])
-                copy.start()
-                sent.append(copy)
-        if k < n_z - 1:
-            from_z = wrap(z + ring(n_z)[k], n_z)
-            att_arrived(1, from_z, x)
-            for m, d in enumerate(ring(n_x)):
-                copy = along_x(1, from_z, x, d, pass_send.at[1, k, m])
-                copy.start()
-                sent.append(copy)
+    pass_on(1)
 
     depth = per_z * HD
 
@@ -347,12 +355,12 @@
 
     for i in [0, *ring(n_z)]:
         b = wrap(z + i, n_z)
-        for d in ring(n_x):
+        for part in range(2):
+            for d in ring(n_x):
+                att_arrived(part, 1, b, wrap(x + d, n_x))
             if i > 0:
-                att_arrived(0, b, wrap(x + d, n_x))
-            att_arrived(1, b, wrap(x + d, n_x))
-        if i > 0:
-            att_arrived(0, b, x)
+                for d in [0, *ring(n_x)]:
+                    att_arrived(part, 0, b, wrap(x + d, n_x))
         left = jnp.concatenate(
             [att[:, b, :, k].reshape(2 * half, HD) for k in range(couples)], axis=1
         )
@@ -452,6 +460,18 @@
         x_send.at[(z * n_attn + a) * per_z + lane], x_recv.at[e, a], xr_sem.at[z]
     )
     own_x.start()
+
+    for copy in sent:
+        copy.wait_send()
+    for q in range(2):
+        push_w(q).wait_send()
+    push_gain.wait_send()
+    for b in range(n_attn):
+        for other in range(CORES):
+            def left_here(b=b, other=other):
+                push_part(b, other).wait_send()
+
+            pl.when(jnp.logical_not((b == a) & (core == other)))(left_here)
 
     squares = jnp.zeros((rows, HD), F32)
     push_gain.wait_recv()
@@ -521,17 +541,6 @@
         back = y_recv[pl.ds(p * n_exp, n_exp)].reshape(slots, HD)
         out[...] += dot(comb_high[p], back) + dot(comb_low[p], back)
 
-    for copy in sent:
-        copy.wait_send()
-    for q in range(2):
-        push_w(q).wait_send()
-    push_gain.wait_send()
-    for b in range(n_attn):
-        for other in range(CORES):
-            def left_here(b=b, other=other):
-                push_part(b, other).wait_send()
-
-            pl.when(jnp.logical_not((b == a) & (core == other)))(left_here)
     for buffer, sem in ((x_send, xs_sem), (y_send, ys_sem)):
         gone = buffer.at[pl.ds(0, experts - 1)]
         pltpu.make_async_copy(gone, gone, sem).wait()
@@ -570,7 +579,7 @@
     sem = pltpu.SemaphoreType.DMA
     return pl.pallas_call(
         functools.partial(layer_kernel, cfg),
-        out_shape=jax.ShapeDtypeStruct(residual.shape, F32),
+        out_shape=pltpu.VMEM(residual.shape, F32),
         in_specs=[anywhere] * 11,
         out_specs=pl.BlockSpec(memory_space=pltpu.VMEM),
         scratch_shapes=[
@@ -607,9 +616,9 @@
             sem((2,)),
             sem,
             sem,
-            sem((2, 2, max(n_x, n_z) - 1)),
-            sem((2, max(n_x, n_z) - 1, max(n_x, n_z) - 1)),
-            sem((2, n_z, n_x)),
+            sem((2, 2, 2, max(n_x, n_z) - 1)),
+            sem((2, 2, max(n_x, n_z) - 1, max(n_x, n_z) - 1)),
+            sem((2, 2, n_z, n_x)),
             sem((n_attn * CORES,)),
             sem((n_attn * CORES,)),
             sem,

time: 48.8 us -> 45.8 us (0.939)
  Pallas kernels: 47.2 us -> 45.1 us
  local copies, waits for them, and re-layouts: 1.47 us -> 0.63 us
    pallas_call x1, Pallas kernels: 47.2 us -> 45.1 us  [body(): pl.pallas_call(functools.partial(layer_kernel, cfg), out_shape=pltpu.VMEM...]
    unnamed x1, local copies, waits for them, and re-layouts: 1.47 us -> 0.63 us
where the time goes in v5:
time: 45.8 us; the launch traced here: 45.7 us
  Pallas kernels  45.1 us (98%)
  local copies, waits for them, and re-layouts  0.63 us (1%)
    pallas_call x1, Pallas kernels, body(): pl.pallas_call(functools.partial(layer_kernel, cfg), out_shape=pltpu.VMEM...  45.1 us

profile of v5, /device:TPU:1, one launch (start us, length us, event | category | flops | bytes accessed | tf_op | source)
XLA Modules:
  0.0 45.7 jit_solution(17557417206386494291)
XLA Ops:
  0.0 45.1 %layer.1 = f32[128,128]{1,0:T(8,128)S(1)} custom-call(s32[16]{0:T(128)} %lengths.1, f32[128,128]{1,0:T(8,128)} %residual.1, bf16[16,2048]{1,0:T(8,128)(2,1)} %queries.1, bf16[16,1024,128]{2,1,0:T(8,128)(2,1)} %keys.1, bf16[16,1024,128]{2,1,0:T(8,128)(2,1)} %values.1, bf16[8,2,128,128]{3,2,1,0:T(8,128)(2,1)} %bitcast.4, f32[1,128]{1,0:T(1,128)} %bitcast.7, ...), custom_call_target="tpu_custom_call" | custom-call | tf_op jit(solution)/shard_map/layer/pallas_call | solution.py:580
  45.1 0.6 %copy.13 = f32[128,128]{1,0:T(8,128)} copy(f32[128,128]{1,0:T(8,128)S(1)} %layer.1) | data formatting | bytes 131072

commit v6 on v5

--- a/solution.py
+++ b/solution.py
@@ -56,8 +56,7 @@
     part_send,
     part_recv,
     select,
-    comb_high,
-    comb_low,
+    comb,
     x_send,
     x_recv,
     gate_up_buf,
@@ -249,8 +248,9 @@
             pl.semaphore_wait(barrier, len(known))
         own_away(part, False)
         if part == 1:
+            own_away(0, True)
             pass_on(0)
-        own_away(part, True)
+            own_away(1, True)
 
     ahead = score(0)
     for g in range(n_group):
@@ -328,8 +328,8 @@
         wide = dot(spread, table)
         here = wide[:, :block] == slot
         select[p] = jnp.where(here, wide[:, block : 2 * block], 0.0).astype(BF16)
-        comb_high[p] = jnp.where(here, wide[:, 2 * block : 3 * block], 0.0).T.astype(BF16)
-        comb_low[p] = jnp.where(here, wide[:, 3 * block :], 0.0).T.astype(BF16)
+        comb[p, :block] = jnp.where(here, wide[:, 2 * block : 3 * block], 0.0).T.astype(BF16)
+        comb[p, block:] = jnp.where(here, wide[:, 3 * block :], 0.0).T.astype(BF16)
 
     for q in range(2):
         load_w(q).wait()
@@ -539,7 +539,8 @@
         arrived = y_recv.at[pl.ds(p * n_exp, n_exp)]
         pltpu.make_async_copy(arrived, arrived, yr_sem.at[p]).wait()
         back = y_recv[pl.ds(p * n_exp, n_exp)].reshape(slots, HD)
-        out[...] += dot(comb_high[p], back) + dot(comb_low[p], back)
+        both = dot(comb[p], back)
+        out[...] += both[:block] + both[block:]
 
     for buffer, sem in ((x_send, xs_sem), (y_send, ys_sem)):
         gone = buffer.at[pl.ds(0, experts - 1)]
@@ -599,8 +600,7 @@
             vmem((n_attn, CORES, half, HD), BF16),
             vmem((n_attn, CORES, half, HD), BF16),
             vmem((n_attn, slots, block), BF16),
-            vmem((n_attn, block, slots), BF16),
-            vmem((n_attn, block, slots), BF16),
+            vmem((n_z, 2 * block, slots), BF16),
             vmem((n_attn * n_exp, CAP, HD), BF16),
             vmem((n_exp, n_attn, CAP, HD), BF16),
             vmem((features, 2 * width), BF16),

time: 45.8 us -> 45.8 us (level)
  no operation moved by 1% of the time
where the time goes in v6:
time: 45.8 us; the launch traced here: 45.7 us
  Pallas kernels  45.1 us (98%)
  local copies, waits for them, and re-layouts  0.63 us (1%)
    pallas_call x1, Pallas kernels, body(): pl.pallas_call(functools.partial(layer_kernel, cfg), out_shape=pltpu.VMEM...  45.1 us

profile of v6, /device:TPU:1, one launch (start us, length us, event | category | flops | bytes accessed | tf_op | source)
XLA Modules:
  0.0 45.7 jit_solution(8811743605591318641)
XLA Ops:
  0.0 45.1 %layer.1 = f32[128,128]{1,0:T(8,128)S(1)} custom-call(s32[16]{0:T(128)} %lengths.1, f32[128,128]{1,0:T(8,128)} %residual.1, bf16[16,2048]{1,0:T(8,128)(2,1)} %queries.1, bf16[16,1024,128]{2,1,0:T(8,128)(2,1)} %keys.1, bf16[16,1024,128]{2,1,0:T(8,128)(2,1)} %values.1, bf16[8,2,128,128]{3,2,1,0:T(8,128)(2,1)} %bitcast.4, f32[1,128]{1,0:T(1,128)} %bitcast.7, ...), custom_call_target="tpu_custom_call" | custom-call | tf_op jit(solution)/shard_map/layer/pallas_call | solution.py:581
  45.1 0.6 %copy.13 = f32[128,128]{1,0:T(8,128)} copy(f32[128,128]{1,0:T(8,128)S(1)} %layer.1) | data formatting | bytes 131072
